TPU v7x, 256 devices: a whole 4x4x8 slice. The times are simulated.
256 devices in a mesh: ctx: 128 (over x_hi, z, y, core), tp: 2 (over x_lo).
Axes of the slice: x: 4 (x_hi: 2, x_lo: 2; x = x_hi * 2 + x_lo), y: 4, z: 8, core: 2. Of those that a mesh axis runs over, the one named last changes fastest.
Arguments:
- query: bfloat16 [32768, 2048], P('ctx', 'tp'), may hold values from -6 to 6
- key_in: bfloat16 [32768, 2048], P('ctx', 'tp'), may hold values from -6 to 6
- value: bfloat16 [32768, 2048], P('ctx', 'tp'), may hold values from -6 to 6
- grad_out: bfloat16 [32768, 2048], P('ctx', 'tp'), may hold values from -6 to 6
- residue: float32 [16, 2048], P(None, 'tp'), may hold values from -0.125 to 0.125
- rate: float32 [16, 2048], P(None, 'tp'), may hold values from 0.5 to 1024
Outputs:
- grad_query: bfloat16 [32768, 2048], P('ctx', 'tp')
- grad_key: bfloat16 [32768, 2048], P('ctx', 'tp')
- grad_value: bfloat16 [32768, 2048], P('ctx', 'tp')
- grad_residue: float32 [16, 2048], P(None, 'tp')
- grad_rate: float32 [16, 2048], P(None, 'tp')
All inputs are finite; a program needn't handle non-finite values.
Results may differ from a plain program's by a relative error of at most 0.0058.
Values may be sent and summed in bfloat16 or wider, within the bound.
A program may use at most 320 MiB of HBM per device.

v0:
```python
from functools import partial

import jax
import jax.numpy as jnp
from jax import lax
from jax.sharding import PartitionSpec as P

BLK = 128


HIGH = lax.Precision.HIGHEST


def combine_fwd(lam, earlier, later):
    span_a, state_a, moment_a = earlier
    span_b, state_b, moment_b = later
    decay = jnp.exp(-lam * span_b)
    return (
        span_a + span_b,
        decay * state_a + state_b,
        decay * (moment_a + span_b * state_a) + moment_b,
    )


def combine_rev(lam, earlier, later):
    span_a, state_a = earlier
    span_b, state_b = later
    return (span_a + span_b, jnp.exp(-lam * span_b) * state_a + state_b)


def layouts():
    return ("cbj", "cbi", "cmb", 2)


def prepare(gated, grad_conv, rate, seq_len):
    lay_j, lay_i, lay_s, axis_b = layouts()
    lam = rate / seq_len
    pos = jnp.arange(BLK, dtype=jnp.float32)[:, None, None]
    head = jnp.exp(-lam * pos)
    head_next = jnp.exp(-lam * (pos + 1.0))
    tail = jnp.exp(-lam * (BLK - 1.0 - pos))
    back = jnp.exp(-lam * (BLK - pos))
    chans, rows = gated.shape
    blocks = rows // BLK
    gated_b = gated.astype(jnp.float32).reshape(chans, blocks, BLK)
    grad_b = grad_conv.astype(jnp.float32).reshape(chans, blocks, BLK)
    lam_s = lam.T[:, :, None]
    spans = jnp.full((1, 1, blocks), float(BLK), jnp.float32)
    state_sum = jnp.einsum(lay_j + ",jmc->" + lay_s, gated_b, tail, precision=HIGH)
    moment_sum = jnp.einsum(
        lay_j + ",jmc->" + lay_s, gated_b, (BLK - 1.0 - pos) * tail, precision=HIGH
    )
    back_sum = jnp.einsum(lay_i + ",imc->" + lay_s, grad_b, head, precision=HIGH)
    fwd_incl = lax.associative_scan(
        partial(combine_fwd, lam_s), (spans, state_sum, moment_sum), axis=axis_b
    )
    rev_incl = lax.associative_scan(
        partial(combine_rev, lam_s), (spans, back_sum), reverse=True, axis=axis_b
    )
    tables = (lam_s, pos, head, head_next, back)
    return (tables, gated_b, grad_b, fwd_incl, rev_incl)


def shift_down(arr, axis_b):
    count = arr.shape[axis_b]
    first = jnp.zeros_like(lax.slice_in_dim(arr, 0, 1, axis=axis_b))
    return jnp.concatenate([first, lax.slice_in_dim(arr, 0, count - 1, axis=axis_b)], axis_b)


def shift_up(arr, axis_b):
    count = arr.shape[axis_b]
    last = jnp.zeros_like(lax.slice_in_dim(arr, 0, 1, axis=axis_b))
    return jnp.concatenate([lax.slice_in_dim(arr, 1, count, axis=axis_b), last], axis_b)


def finish(tables, gated_b, grad_b, fwd_incl, rev_incl, fwd_in, rev_in, residue, seq_len):
    lam_s, pos, head, head_next, back = tables
    lay_j, lay_i, lay_s, axis_b = layouts()
    fwd_excl = tuple((shift_down(part, axis_b) for part in fwd_incl))
    rev_excl = tuple((shift_up(part, axis_b) for part in rev_incl))
    _, state_in, moment_in = combine_fwd(lam_s, fwd_in, fwd_excl)
    _, back_in = combine_rev(lam_s, rev_in, rev_excl)
    lag = jnp.arange(BLK)
    onehot = (lag[:, None, None] - lag[None, :, None] == lag[None, None, :]).astype(jnp.float32)
    short_filter = jnp.einsum("mc,kmc->kc", residue, head, precision=HIGH)
    toeplitz = jnp.einsum("kc,ijk->cij", short_filter, onehot, precision=HIGH)
    conv = jnp.einsum("cij," + lay_j + "->" + lay_i, toeplitz, gated_b, precision=HIGH)
    conv = conv + jnp.einsum(
        "imc," + lay_s + "->" + lay_i, residue * head_next, state_in, precision=HIGH
    )
    grad_gated = jnp.einsum("cij," + lay_i + "->" + lay_j, toeplitz, grad_b, precision=HIGH)
    grad_gated = grad_gated + jnp.einsum(
        "jmc," + lay_s + "->" + lay_j, residue * back, back_in, precision=HIGH
    )
    outer = jnp.einsum(lay_i + "," + lay_j + "->cij", grad_b, gated_b, precision=HIGH)
    correl = jnp.einsum("cij,ijk->kc", outer, onehot, precision=HIGH)
    near_w = jnp.einsum(lay_i + ",imc->" + lay_s, grad_b, head_next, precision=HIGH)
    near_t = jnp.einsum(lay_i + ",imc->" + lay_s, grad_b, (pos + 1.0) * head_next, precision=HIGH)
    pair = lay_s + "," + lay_s + "->mc"
    grad_residue = jnp.einsum("kc,kmc->mc", correl, head, precision=HIGH)
    grad_residue = grad_residue + jnp.einsum(pair, near_w, state_in, precision=HIGH)
    weighted = jnp.einsum("kc,kmc->mc", correl, pos * head, precision=HIGH)
    weighted = weighted + jnp.einsum(pair, near_t, state_in, precision=HIGH)
    weighted = weighted + jnp.einsum(pair, near_w, moment_in, precision=HIGH)
    grad_rate = -residue / seq_len * weighted
    scale = seq_len ** (-0.5)
    chans = conv.shape[0]
    rows = conv.shape[1] * BLK
    shape_out = (chans, rows)
    return (
        conv.reshape(shape_out).astype(jnp.bfloat16),
        grad_gated.reshape(shape_out).astype(jnp.bfloat16),
        scale * grad_residue,
        scale * grad_rate,
    )


def local(query, key_in, value, grad_out, residue, rate):
    gated = (key_in.astype(jnp.float32) * value.astype(jnp.float32)).astype(jnp.bfloat16)
    grad_conv = (grad_out.astype(jnp.float32) * query.astype(jnp.float32)).astype(jnp.bfloat16)
    gated_t = gated.T
    grad_t = grad_conv.T
    gated_ch, grad_ch = (
        lax.all_to_all(gated_t, "ctx", split_axis=0, concat_axis=1, tiled=True),
        lax.all_to_all(grad_t, "ctx", split_axis=0, concat_axis=1, tiled=True),
    )
    chans = gated_ch.shape[0]
    seq_len = gated_ch.shape[1]
    start = lax.axis_index("ctx") * chans
    residue_ch = lax.dynamic_slice_in_dim(residue, start, chans, 1)
    rate_ch = lax.dynamic_slice_in_dim(rate, start, chans, 1)
    tables, gated_b, grad_b, fwd_incl, rev_incl = prepare(gated_ch, grad_ch, rate_ch, seq_len)
    zero_span = jnp.zeros((1, 1, 1), jnp.float32)
    zero_state = jnp.zeros((1, 1, 1), jnp.float32)
    conv_ch, grad_gated_ch, own_res, own_rate = finish(
        tables,
        gated_b,
        grad_b,
        fwd_incl,
        rev_incl,
        (zero_span, zero_state, zero_state),
        (zero_span, zero_state),
        residue_ch,
        seq_len,
    )
    conv_t, grad_gated_t = (
        lax.all_to_all(conv_ch, "ctx", split_axis=1, concat_axis=0, tiled=True),
        lax.all_to_all(grad_gated_ch, "ctx", split_axis=1, concat_axis=0, tiled=True),
    )
    conv = conv_t.T
    grad_gated = grad_gated_t.T
    grad_residue, grad_rate = (
        lax.all_gather(own_res, "ctx", axis=1, tiled=True),
        lax.all_gather(own_rate, "ctx", axis=1, tiled=True),
    )
    conv_f = conv.astype(jnp.float32)
    grad_gated_f = grad_gated.astype(jnp.float32)
    grad_query = (grad_out.astype(jnp.float32) * conv_f).astype(jnp.bfloat16)
    grad_key = (grad_gated_f * value.astype(jnp.float32)).astype(jnp.bfloat16)
    grad_value = (grad_gated_f * key_in.astype(jnp.float32)).astype(jnp.bfloat16)
    return (grad_query, grad_key, grad_value, grad_residue, grad_rate)


def solution(mesh):
    in_specs = (
        P("ctx", "tp"),
        P("ctx", "tp"),
        P("ctx", "tp"),
        P("ctx", "tp"),
        P(None, "tp"),
        P(None, "tp"),
    )
    out_specs = (P("ctx", "tp"), P("ctx", "tp"), P("ctx", "tp"), P(None, "tp"), P(None, "tp"))
    return jax.shard_map(local, mesh=mesh, in_specs=in_specs, out_specs=out_specs, check_vma=False)
```

profile of v0, /device:TPU:1, one launch (start us, length us, event | category | flops | bytes accessed | tf_op | source)
XLA Modules:
  0.0 864.4 jit_solution(11036327460467527053)
XLA Ops:
  3.1 17.0 %all-to-all-start.2 = ((bf16[128,8,256]{2,1,0:T(8,128)(2,1)}), bf16[128,8,256]{2,1,0:T(8,128)(2,1)S(1)}, u32[]{:S(2)}, u32[]{:S(2)}) async-start(bf16[128,8,256]{2,1,0:T(8,128)(2,1)} %fusion.14), calls=%async_computation.2 | async-start | bytes 1048576 | tf_op jit(solution)/shard_map/all_to_all | solution.py:125
  21.5 6.5 fusion.1
  28.0 14.1 %all-to-all-done.2 = bf16[128,8,256]{2,1,0:T(8,128)(2,1)S(1)} async-done(((bf16[128,8,256]{2,1,0:T(8,128)(2,1)}), bf16[128,8,256]{2,1,0:T(8,128)(2,1)S(1)}, u32[]{:S(2)}, u32[]{:S(2)}) %all-to-all-start.2) | async-done | bytes 524320 | tf_op jit(solution)/shard_map/all_to_all | solution.py:125
  42.9 2.2 slice.423
  53.7 44.0 %pad.368 = f32[8,16,256]{1,0,2:T(8,128)S(1)} pad(f32[8,16,128]{1,0,2:T(8,128)} %add.470, f32[]{:T(128)} %constant.112.clone.1), padding=0_0_0x0_0_0x1_0_1 | pad | bytes 196612
  102.6 44.0 %pad.279 = f32[8,16,255]{1,0,2:T(8,128)S(1)} pad(f32[8,16,128]{1,0,2:T(8,128)} %pad_maximum_fusion.1, f32[]{:T(128)} %constant.112.clone.1), padding=0_0_0x0_0_0x0_0_1 | pad | bytes 196100 | tf_op jit(solution)/shard_map/slice | solution.py:73
  152.5 5.8 all-to-all-start.3
  159.5 20.9 %all-to-all-done.3 = bf16[8,128,256]{2,0,1:T(8,128)(2,1)S(1)} async-done(((bf16[8,128,256]{2,0,1:T(8,128)(2,1)}), bf16[8,128,256]{2,0,1:T(8,128)(2,1)S(1)}, u32[]{:S(2)}, u32[]{:S(2)}) %all-to-all-start.3) | async-done | bytes 524320 | tf_op jit(solution)/shard_map/all_to_all | solution.py:148
  182.6 5.5 all-to-all-start
  193.9 16.3 %all-to-all-done = bf16[128,8,256]{2,1,0:T(8,128)(2,1)S(1)} async-done(((bf16[128,8,256]{2,1,0:T(8,128)(2,1)}), bf16[128,8,256]{2,1,0:T(8,128)(2,1)S(1)}, u32[]{:S(2)}, u32[]{:S(2)}) %all-to-all-start) | async-done | bytes 524320 | tf_op jit(solution)/shard_map/all_to_all | solution.py:124
  211.1 2.2 slice.385
  245.2 3.1 pad.188
  248.4 3.1 pad.189
  252.8 3.1 pad.220
  256.0 3.1 pad.221
  266.4 4.6 pad.190
  270.9 4.5 pad.191
  275.5 4.6 pad.223
  281.4 4.5 pad.222
  291.9 5.5 pad.193
  298.8 8.3 pad.224
  307.1 8.3 pad.225
  320.1 10.9 %pad.227 = f32[8,16,64]{1,0,2:T(8,128)S(1)} pad(f32[8,16,32]{1,0,2:T(8,128)} %add.505, f32[]{:T(128)} %constant.112.clone.1), padding=0_0_0x0_0_0x1_0_1 | pad | bytes 49156 | tf_op jit(solution)/shard_map/pad | solution.py:54
  332.5 15.0 %pad.226 = f32[8,16,64]{1,0,2:T(8,128)} pad(f32[8,16,32]{1,0,2:T(8,128)} %pad_maximum_fusion.8, f32[]{:T(128)} %constant.112.clone.1), padding=0_0_0x0_0_0x0_1_1 | pad | bytes 49156 | tf_op jit(solution)/shard_map/pad | solution.py:54
  353.9 3.1 slice.500
  361.3 38.7 %pad.369 = f32[8,16,256]{1,0,2:T(8,128)} pad(f32[8,16,128]{1,0,2:T(8,128)S(1)} %add.511, f32[]{:T(128)} %constant.112.clone.1), padding=0_0_0x0_0_0x1_0_1 | pad | bytes 196612
  405.1 38.7 %pad.281 = f32[8,16,255]{1,0,2:T(8,128)} pad(f32[8,16,128]{1,0,2:T(8,128)S(1)} %pad_maximum_fusion.2, f32[]{:T(128)} %constant.112.clone.1), padding=0_0_0x0_0_0x0_0_1 | pad | bytes 196100 | tf_op jit(solution)/shard_map/slice | solution.py:67
  445.0 38.7 %pad.277 = f32[8,16,255]{1,0,2:T(8,128)} pad(f32[8,16,128]{1,0,2:T(8,128)S(1)} %pad_maximum_fusion, f32[]{:T(128)} %constant.112.clone.1), padding=0_0_0x0_0_0x0_0_1 | pad | bytes 196100 | tf_op jit(solution)/shard_map/slice | solution.py:67
  483.7 3.4 fusion
  491.5 5.7 all-to-all-start.1
  499.8 184.7 %all_gather.7 = f32[16,1024]{0,1:T(8,128)S(1)} all-gather(f32[16,8]{0,1:T(8,128)S(1)} %multiply_multiply_fusion), channel_id=1, replica_groups=mesh['ctx'=128,'tp'=2] {'ctx'}, dimensions={1}, use_global_device_ids=true | all-gather | bytes 66048 | tf_op jit(solution)/shard_map/all_gather | solution.py:154
  685.6 176.6 %all_gather.6 = f32[16,1024]{0,1:T(8,128)S(1)} all-gather(f32[16,8]{0,1:T(8,128)S(1)} %add_multiply_fusion.6), channel_id=1, replica_groups=mesh['ctx'=128,'tp'=2] {'ctx'}, dimensions={1}, use_global_device_ids=true | all-gather | bytes 66048 | tf_op jit(solution)/shard_map/all_gather | solution.py:153
  (292 shorter events, 115.4 us)
Async XLA Ops:
  3.1 39.0 %all-to-all-start.2 = ((bf16[128,8,256]{2,1,0:T(8,128)(2,1)}), bf16[128,8,256]{2,1,0:T(8,128)(2,1)S(1)}, u32[]{:S(2)}, u32[]{:S(2)}) async-start(bf16[128,8,256]{2,1,0:T(8,128)(2,1)} %fusion.14), calls=%async_computation.2 | async-start | bytes 1048576 | tf_op jit(solution)/shard_map/all_to_all | solution.py:125
  21.1 129.0 %copy-start.39 = (f32[16,8]{0,1:T(8,128)}, f32[16,8]{0,1:T(8,128)S(1)}, u32[]{:S(2)}) copy-start(f32[16,8]{0,1:T(8,128)S(1)} %copy.254) | copy-start | bytes 1540
  21.1 6.9 copy-start.41
  21.1 128.5 %copy-start.37 = (f32[8,16]{1,0:T(8,128)}, f32[8,16]{1,0:T(8,128)S(1)}, u32[]{:S(2)}) copy-start(f32[8,16]{1,0:T(8,128)S(1)} %get-tuple-element.84) | copy-start | bytes 1540
  21.4 26.6 %copy-start.43 = (f32[8,16]{1,0:T(8,128)}, f32[8,16]{1,0:T(8,128)S(1)}, u32[]{:S(2)}) copy-start(f32[8,16]{1,0:T(8,128)S(1)} %get-tuple-element.86) | copy-start | bytes 1540
  21.4 26.8 %copy-start.35 = (f32[8,16]{1,0:T(8,128)}, f32[8,16]{1,0:T(8,128)S(1)}, u32[]{:S(2)}) copy-start(f32[8,16]{1,0:T(8,128)S(1)} %get-tuple-element.87) | copy-start | bytes 1540
  21.4 26.9 %copy-start.33 = (f32[8,16]{1,0:T(8,128)}, f32[8,16]{1,0:T(8,128)S(1)}, u32[]{:S(2)}) copy-start(f32[8,16]{1,0:T(8,128)S(1)} %get-tuple-element.88) | copy-start | bytes 1540
  21.4 27.1 %copy-start.31 = (f32[8,16]{1,0:T(8,128)}, f32[8,16]{1,0:T(8,128)S(1)}, u32[]{:S(2)}) copy-start(f32[8,16]{1,0:T(8,128)S(1)} %get-tuple-element.89) | copy-start | bytes 1540
  21.5 27.4 %copy-start.28 = (f32[8,16]{1,0:T(8,128)}, f32[8,16]{1,0:T(8,128)S(1)}, u32[]{:S(2)}) copy-start(f32[8,16]{1,0:T(8,128)S(1)} %get-tuple-element.90) | copy-start | bytes 1540
  49.5 2.3 slice-start
  151.4 6.9 copy-start.22
  152.5 6.0 copy-start.23
  152.5 27.9 %all-to-all-start.3 = ((bf16[8,128,256]{2,0,1:T(8,128)(2,1)}), bf16[8,128,256]{2,0,1:T(8,128)(2,1)S(1)}, u32[]{:S(2)}, u32[]{:S(2)}) async-start(bf16[8,128,256]{2,0,1:T(8,128)(2,1)} %copy.217), calls=%async_computation.3 | async-start | bytes 1048576 | tf_op jit(solution)/shard_map/all_to_all | solution.py:148
  182.6 27.6 %all-to-all-start = ((bf16[128,8,256]{2,1,0:T(8,128)(2,1)}), bf16[128,8,256]{2,1,0:T(8,128)(2,1)S(1)}, u32[]{:S(2)}, u32[]{:S(2)}) async-start(bf16[128,8,256]{2,1,0:T(8,128)(2,1)} %get-tuple-element.53), calls=%async_computation | async-start | bytes 1048576 | tf_op jit(solution)/shard_map/all_to_all | solution.py:124
  188.1 2.5 copy-start.47
  211.1 146.0 %copy-start.11 = (f32[8,16,256]{2,1,0:T(8,128)}, f32[8,16,256]{2,1,0:T(8,128)S(1)}, u32[]{:S(2)}) copy-start(f32[8,16,256]{2,1,0:T(8,128)S(1)} %fusion.39) | copy-start | bytes 393220
  216.1 6.7 copy-start.12
  226.7 2.5 copy-start.26
  226.7 3.1 copy-start.27
  287.4 28.6 %copy-start.30 = (f32[8,16]{1,0:T(8,128)S(1)}, f32[8,16]{1,0:T(8,128)}, u32[]{:S(2)}) copy-start(f32[8,16]{1,0:T(8,128)} %copy-done.28) | copy-start | bytes 1540
  315.4 2.3 copy-start.13
  315.4 2.3 copy-start.14
  315.4 4.2 copy-start.46
  317.7 2.1 copy-start.20
  351.7 6.5 copy-start.8
  361.3 38.7 %copy-start.17 = (f32[8,16,63]{1,0,2:T(8,128)S(1)}, f32[8,16,63]{1,0,2:T(8,128)}, u32[]{:S(2)}) copy-start(f32[8,16,63]{1,0,2:T(8,128)} %get-tuple-element.46) | copy-start | bytes 96772
  405.1 38.8 %copy-start.6 = (f32[8,16,128]{1,0,2:T(8,128)S(1)}, f32[8,16,128]{1,0,2:T(8,128)}, u32[]{:S(2)}) copy-start(f32[8,16,128]{1,0,2:T(8,128)} %add.444) | copy-start | bytes 196612
  444.9 38.8 %copy-start.19 = (f32[8,128,128]{2,1,0:T(8,128)S(1)}, f32[8,128,128]{2,1,0:T(8,128)}, u32[]{:S(2)}) copy-start(f32[8,128,128]{2,1,0:T(8,128)} %fusion.83) | copy-start | bytes 1572868
  444.9 38.8 %copy-start.42 = (s32[128,128]{1,0:T(8,128)S(1)}, s32[128,128]{1,0:T(8,128)}, u32[]{:S(2)}) copy-start(s32[128,128]{1,0:T(8,128)} %copy-done.41) | copy-start | bytes 196612
  483.7 3.4 copy-start.4
  490.4 6.8 copy-start.3
  491.5 371.5 %all-to-all-start.1 = ((bf16[8,128,256]{2,0,1:T(8,128)(2,1)}), bf16[8,128,256]{2,0,1:T(8,128)(2,1)S(1)}, u32[]{:S(2)}, u32[]{:S(2)}) async-start(bf16[8,128,256]{2,0,1:T(8,128)(2,1)} %copy.208), calls=%async_computation.1 | async-start | bytes 1048576 | tf_op jit(solution)/shard_map/all_to_all | solution.py:147
  (26 other events, 30.6 us)
where the time goes:
time: 876 us; the launch traced here: 864 us
  blocking collectives  361 us (41%)
  local copies, waits for them, and re-layouts  348 us (40%)
  waiting for transfers between devices  51.4 us (6%)
  other arithmetic  48.1 us (5%)
  starting transfers between devices  34 us (4%)
  matrix products  19.2 us (2%)
    all_gather x1, blocking collectives, local(): lax.all_gather(own_rate, 'ctx', axis=1, tiled=True)  185 us
    all_gather x1, blocking collectives, local(): lax.all_gather(own_res, 'ctx', axis=1, tiled=True)  177 us
    unnamed x130, local copies, waits for them, and re-layouts  104 us
    pad x24, local copies, waits for them, and re-layouts, prepare(): lax.associative_scan(partial(combine_fwd, lam_s), (spans, state_sum, mome...  88.6 us
    slice x2, local copies, waits for them, and re-layouts, shift_down(): lax.slice_in_dim(arr, 0, count - 1, axis=axis_b)  77.4 us
    slice x2, local copies, waits for them, and re-layouts, shift_up(): lax.slice_in_dim(arr, 1, count, axis=axis_b)  45.3 us
    all_to_all x1, waiting for transfers between devices, local(): lax.all_to_all(grad_gated_ch, 'ctx', split_axis=1, concat_axis=0, tiled=T...  20.9 us
    slice x20, local copies, waits for them, and re-layouts, prepare(): lax.associative_scan(partial(combine_fwd, lam_s), (spans, state_sum, mome...  20.2 us
  transfers between devices with their start and end apart: 4, of which 3 were waited for; matrix products, arithmetic and copies ran while one was open for 2% of the time, Pallas kernels for 0%

commit v1 on v0

v1 whole, which is shorter than its diff:
```python
import jax
import jax.numpy as jnp
from jax import lax
from jax.experimental import pallas as pl
from jax.experimental.pallas import tpu as pltpu
from jax.sharding import PartitionSpec as P

SEQ = 32768
MODES = 16
ROWS = 256
SUB = 16
NSUB = ROWS // SUB
LANES = 128
TILE = 256
INNER = 8
OUTER = 16
F32 = jnp.float32
BF16 = jnp.bfloat16


def rows_iota(shape, dim):
    return lax.broadcasted_iota(jnp.int32, shape, dim)


def dot(a, b):
    return jnp.dot(a, b, preferred_element_type=F32)


def gate(a_ref, b_ref):
    return (a_ref[...].astype(F32) * b_ref[...].astype(F32)).astype(BF16)


def state_kernel(q_ref, k_ref, v_ref, go_ref, rate_ref, sub_s_ref, sub_b_ref, send_ref, ptab, btab, uf, gf):
    u = gate(k_ref, v_ref)
    g = gate(go_ref, q_ref)
    for half in range(TILE // LANES):
        cols = slice(half * LANES, (half + 1) * LANES)
        uf[half] = u[:, cols].astype(F32)
        gf[half] = g[:, cols].astype(F32)
    lam = rate_ref[...] * (1.0 / SEQ)
    pos = rows_iota((SUB, TILE), 0).astype(F32)
    for m in range(MODES):
        row = lam[m : m + 1, :]
        ptab[m] = jnp.exp(-row * (SUB - 1.0 - pos)).astype(BF16)
        btab[m] = jnp.exp(-row * (pos + 1.0)).astype(BF16)
    out_row = rows_iota((2 * MODES, MODES * SUB), 0)
    in_row = rows_iota((2 * MODES, MODES * SUB), 1)
    hit = (in_row // SUB) == (out_row % MODES)
    off = (in_row % SUB).astype(F32)
    first = out_row < MODES
    sel_s = jnp.where(hit, jnp.where(first, 1.0, SUB - 1.0 - off), 0.0).astype(BF16)
    sel_b = jnp.where(hit, jnp.where(first, 1.0, off + 1.0), 0.0).astype(BF16)
    step = jnp.exp(-lam * SUB)
    zero = jnp.zeros((MODES, TILE), F32)
    s, q, bn, tn, gr, gw = zero, zero, zero, zero, zero, zero
    decay = jnp.ones((MODES, TILE), F32)
    for k in range(NSUB):
        uk = u[k * SUB : (k + 1) * SUB, :]
        gk = g[k * SUB : (k + 1) * SUB, :]
        su = dot(sel_s, (ptab[...] * uk[None]).reshape(MODES * SUB, TILE))
        sg = dot(sel_b, (btab[...] * gk[None]).reshape(MODES * SUB, TILE))
        s_k, m_k = su[:MODES], su[MODES:]
        b_k, t_k = sg[:MODES], sg[MODES:]
        sub_s_ref[k] = s_k.astype(BF16)
        sub_b_ref[k] = b_k.astype(BF16)
        gr = gr + b_k * s
        gw = gw + t_k * s + b_k * q
        q = step * (q + float(SUB) * s) + m_k
        s = step * s + s_k
        db = decay * b_k
        bn = bn + db
        tn = tn + decay * t_k + float(k * SUB) * db
        decay = decay * step
    halves = []
    for half in range(TILE // LANES):
        acc = [jnp.zeros((8, LANES), F32) for _ in range(SUB)]
        for octet in range(NSUB // 8):
            us = [uf[half, pl.ds(octet * 8 * SUB + b, 8, stride=SUB), :] for b in range(SUB)]
            for b in range(SUB):
                gb = gf[half, pl.ds(octet * 8 * SUB + b, 8, stride=SUB), :]
                for lag in range(b + 1):
                    acc[lag] = acc[lag] + gb * us[b - lag]
        halves.append([jnp.sum(a, axis=0, keepdims=True) for a in acc])
    unit = jnp.exp(-lam)
    power = jnp.ones((MODES, TILE), F32)
    for lag in range(SUB):
        row = jnp.concatenate([h[lag] for h in halves], axis=1)
        term = row * power
        gr = gr + term
        gw = gw + float(lag) * term
        power = power * unit
    for half in range(TILE // LANES):
        cols = slice(half * LANES, (half + 1) * LANES)
        for n, part in enumerate((s, q, bn, tn, gr, gw)):
            send_ref[half, n * MODES : (n + 1) * MODES, :] = part[:, cols].astype(BF16)


def exchange_kernel(
    send_a, rate_ref, out_ref,
    recv_a, send_b, recv_b, send_d, recv_d, send_c, recv_c, pre_s, pre_b,
    sa, ra, sb, rb, sd, rd, sc, rc,
):
    me = lax.axis_index("ctx")
    grp = me // INNER
    idx = me % INNER
    inner = [(idx + d) % INNER for d in range(1, INNER)]
    outer = [(grp + d) % OUTER for d in range(1, OUTER)]

    def to_inner(j):
        return {"ctx": grp * INNER + j}

    def to_outer(p):
        return {"ctx": p * INNER + idx}

    barrier = pltpu.get_barrier_semaphore()
    for j in inner:
        pl.semaphore_signal(barrier, inc=1, device_id=to_inner(j), device_id_type=pl.DeviceIdType.MESH)
    for p in outer:
        pl.semaphore_signal(barrier, inc=1, device_id=to_outer(p), device_id_type=pl.DeviceIdType.MESH)
    pl.semaphore_wait(barrier, INNER + OUTER - 2)

    def trade(src, dst, ssem, rsem, own, others, target):
        for j in others:
            pltpu.make_async_remote_copy(
                src_ref=src.at[j], dst_ref=dst.at[own], send_sem=ssem.at[j], recv_sem=rsem.at[own],
                device_id=target(j), device_id_type=pl.DeviceIdType.MESH,
            ).start()
        dst[own] = src[own]
        for j in others:
            cp = pltpu.make_async_remote_copy(
                src_ref=src.at[j], dst_ref=dst.at[j], send_sem=ssem.at[j], recv_sem=rsem.at[j],
                device_id=target(j), device_id_type=pl.DeviceIdType.MESH,
            )
            cp.wait_recv()

    def drain(src, dst, ssem, rsem, others, target):
        for j in others:
            pltpu.make_async_remote_copy(
                src_ref=src.at[j], dst_ref=dst.at[j], send_sem=ssem.at[j], recv_sem=rsem.at[j],
                device_id=target(j), device_id_type=pl.DeviceIdType.MESH,
            ).wait_send()

    trade(send_a, recv_a, sa, ra, idx, inner, to_inner)
    cols = pl.ds(pl.multiple_of(idx * LANES, LANES), LANES)
    lam = rate_ref[:, cols] * (1.0 / SEQ)
    dec = jnp.exp(-lam * float(ROWS))
    zero = jnp.zeros((MODES, LANES), F32)
    s, q, gr, gw, bn, tn = zero, zero, zero, zero, zero, zero
    front = jnp.ones((MODES, LANES), F32)
    nears = []
    for j in range(INNER):
        part = [recv_a[j, n * MODES : (n + 1) * MODES, :].astype(F32) for n in range(6)]
        s_j, m_j, b_j, t_j, gr_j, gw_j = part
        pre_s[j] = s
        nears.append(b_j)
        gr = gr + gr_j + b_j * s
        gw = gw + gw_j + t_j * s + b_j * q
        q = dec * (q + float(ROWS) * s) + m_j
        s = dec * s + s_j
        db = front * b_j
        bn = bn + db
        tn = tn + front * t_j + float(ROWS * j) * db
        front = front * dec
    back = zero
    for j in reversed(range(INNER)):
        pre_b[j] = back
        back = dec * back + nears[j]
    for n, part in enumerate((s, q, bn, tn, gr, gw)):
        send_b[:, n, :] = part

    trade(send_b, recv_b, sb, rb, grp, outer, to_outer)
    mine = rows_iota((MODES, LANES), 0) == grp
    lam_row = jnp.sum(jnp.where(mine, lam, 0.0), axis=0, keepdims=True)
    span = float(ROWS * INNER)
    dec_g = jnp.exp(-lam_row * span)
    zrow = jnp.zeros((1, LANES), F32)
    s, q, gr, gw, back = zrow, zrow, zrow, zrow, zrow
    for p in range(OUTER):
        s_p, m_p, b_p, t_p, gr_p, gw_p = [recv_b[p, n : n + 1, :] for n in range(6)]
        send_d[p, 0:1, :] = s
        gr = gr + gr_p + b_p * s
        gw = gw + gw_p + t_p * s + b_p * q
        q = dec_g * (q + span * s) + m_p
        s = dec_g * s + s_p
    for p in reversed(range(OUTER)):
        send_d[p, 1:2, :] = back
        send_d[p, 2:3, :] = gr
        send_d[p, 3:4, :] = gw
        back = dec_g * back + recv_b[p, 2:3, :]

    trade(send_d, recv_d, sd, rd, grp, outer, to_outer)
    state, back, gr, gw = [recv_d[:, n, :] for n in range(4)]
    decs = [jnp.ones((MODES, LANES), F32)]
    for j in range(1, INNER):
        decs.append(decs[-1] * dec)
    for j in range(INNER):
        parts = (pre_s[j] + decs[j] * state, pre_b[j] + decs[INNER - 1 - j] * back, gr, gw)
        for n, part in enumerate(parts):
            send_c[j, n * MODES : (n + 1) * MODES, :] = part.astype(BF16)

    trade(send_c, recv_c, sc, rc, idx, inner, to_inner)
    out_ref[...] = recv_c[...]
    drain(send_a, recv_a, sa, ra, inner, to_inner)
    drain(send_b, recv_b, sb, rb, outer, to_outer)
    drain(send_d, recv_d, sd, rd, outer, to_outer)
    drain(send_c, recv_c, sc, rc, inner, to_inner)


def finish_kernel(
    q_ref, k_ref, v_ref, go_ref, res_ref, rate_ref, sub_s_ref, sub_b_ref, in_ref,
    gq_ref, gk_ref, gv_ref, gres_ref, grate_ref, wtab, vtab, htab,
):
    u = gate(k_ref, v_ref)
    g = gate(go_ref, q_ref)
    lam = rate_ref[...] * (1.0 / SEQ)
    res = res_ref[...]

    def incoming(n):
        return jnp.concatenate(
            [in_ref[h, n * MODES : (n + 1) * MODES, :].astype(F32) for h in range(TILE // LANES)], axis=1
        )

    scale = SEQ ** -0.5
    gres_ref[...] = scale * incoming(2)
    grate_ref[...] = (-scale / SEQ) * res * incoming(3)
    unit = jnp.exp(-lam)
    power = res
    for b in range(SUB):
        htab[b] = jnp.broadcast_to(jnp.sum(power, axis=0, keepdims=True), (SUB, TILE)).astype(BF16)
        vtab[SUB - 1 - b] = power.astype(BF16)
        power = power * unit
        wtab[b] = power.astype(BF16)
    step = jnp.exp(-lam * SUB)
    state = incoming(0)
    states = []
    for k in range(NSUB):
        states.append(state.astype(BF16))
        state = step * state + sub_s_ref[k].astype(F32)
    back = incoming(1)
    backs = [None] * NSUB
    for k in reversed(range(NSUB)):
        backs[k] = back.astype(BF16)
        back = step * back + sub_b_ref[k].astype(F32)
    out_row = rows_iota((SUB, SUB * SUB), 0)
    in_row = rows_iota((SUB, SUB * SUB), 1)
    major, minor = in_row // SUB, in_row % SUB
    pick = (major == out_row).astype(F32).astype(BF16)
    down = (major + minor == out_row).astype(F32).astype(BF16)
    up = (minor - major == out_row).astype(F32).astype(BF16)
    for k in range(NSUB):
        rows = slice(k * SUB, (k + 1) * SUB)

        def spread(tab, val):
            return (tab[...] * val[None]).reshape(SUB * SUB, TILE)

        conv = dot(pick, spread(wtab, states[k])) + dot(down, spread(htab, u[rows]))
        grad = dot(pick, spread(vtab, backs[k])) + dot(up, spread(htab, g[rows]))
        gq_ref[rows, :] = (go_ref[rows, :].astype(F32) * conv).astype(BF16)
        gk_ref[rows, :] = (v_ref[rows, :].astype(F32) * grad).astype(BF16)
        gv_ref[rows, :] = (k_ref[rows, :].astype(F32) * grad).astype(BF16)


def local(query, key_in, value, grad_out, residue, rate):
    rows, chans = query.shape
    tiles = chans // TILE
    per = TILE // LANES
    big = pl.BlockSpec((ROWS, TILE), lambda i: (0, i))
    small = pl.BlockSpec((MODES, TILE), lambda i: (0, i))
    subs = pl.BlockSpec((NSUB, MODES, TILE), lambda i: (0, 0, i))
    vmem = pl.BlockSpec(memory_space=pltpu.VMEM)
    sub_s, sub_b, summary = pl.pallas_call(
        state_kernel,
        grid=(tiles,),
        out_shape=(
            jax.ShapeDtypeStruct((NSUB, MODES, chans), BF16),
            jax.ShapeDtypeStruct((NSUB, MODES, chans), BF16),
            jax.ShapeDtypeStruct((INNER, 6 * MODES, LANES), BF16),
        ),
        in_specs=[big, big, big, big, small],
        out_specs=[subs, subs, pl.BlockSpec((per, 6 * MODES, LANES), lambda i: (i, 0, 0))],
        scratch_shapes=[
            pltpu.VMEM((MODES, SUB, TILE), BF16),
            pltpu.VMEM((MODES, SUB, TILE), BF16),
            pltpu.VMEM((per, ROWS, LANES), F32),
            pltpu.VMEM((per, ROWS, LANES), F32),
        ],
        compiler_params=pltpu.CompilerParams(vmem_limit_bytes=32 * 2**20),
        name="states",
    )(query, key_in, value, grad_out, rate)

    dma = pltpu.SemaphoreType.DMA
    incoming = pl.pallas_call(
        exchange_kernel,
        out_shape=jax.ShapeDtypeStruct((INNER, 4 * MODES, LANES), BF16),
        in_specs=[vmem, vmem],
        out_specs=vmem,
        scratch_shapes=[
            pltpu.VMEM((INNER, 6 * MODES, LANES), BF16),
            pltpu.VMEM((OUTER, 8, LANES), F32),
            pltpu.VMEM((OUTER, 8, LANES), F32),
            pltpu.VMEM((OUTER, 8, LANES), F32),
            pltpu.VMEM((OUTER, 8, LANES), F32),
            pltpu.VMEM((INNER, 4 * MODES, LANES), BF16),
            pltpu.VMEM((INNER, 4 * MODES, LANES), BF16),
            pltpu.VMEM((INNER, MODES, LANES), F32),
            pltpu.VMEM((INNER, MODES, LANES), F32),
            dma((INNER,)), dma((INNER,)), dma((OUTER,)), dma((OUTER,)),
            dma((OUTER,)), dma((OUTER,)), dma((INNER,)), dma((INNER,)),
        ],
        compiler_params=pltpu.CompilerParams(collective_id=0, has_side_effects=True, vmem_limit_bytes=16 * 2**20),
        name="exchange",
    )(summary, rate)

    return pl.pallas_call(
        finish_kernel,
        grid=(tiles,),
        out_shape=(
            jax.ShapeDtypeStruct((rows, chans), BF16),
            jax.ShapeDtypeStruct((rows, chans), BF16),
            jax.ShapeDtypeStruct((rows, chans), BF16),
            jax.ShapeDtypeStruct((MODES, chans), F32),
            jax.ShapeDtypeStruct((MODES, chans), F32),
        ),
        in_specs=[big, big, big, big, small, small, subs, subs,
                  pl.BlockSpec((per, 4 * MODES, LANES), lambda i: (i, 0, 0))],
        out_specs=[big, big, big, small, small],
        scratch_shapes=[
            pltpu.VMEM((SUB, MODES, TILE), BF16),
            pltpu.VMEM((SUB, MODES, TILE), BF16),
            pltpu.VMEM((SUB, SUB, TILE), BF16),
        ],
        compiler_params=pltpu.CompilerParams(vmem_limit_bytes=32 * 2**20),
        name="finish",
    )(query, key_in, value, grad_out, residue, rate, sub_s, sub_b, incoming)


def solution(mesh):
    big, small = P("ctx", "tp"), P(None, "tp")
    return jax.shard_map(
        local, mesh=mesh, in_specs=(big, big, big, big, small, small),
        out_specs=(big, big, big, small, small), check_vma=False,
    )
```

time: 876 us -> 51.5 us (0.06); the launches traced: 864 us -> 51.2 us
  blocking collectives: 361 us -> 0 us
  local copies, waits for them, and re-layouts: 348 us -> 5 us
  waiting for transfers between devices: 51.4 us -> 0 us
  other arithmetic: 48.1 us -> 0 us
  Pallas kernels: 0 us -> 45.5 us
  starting transfers between devices: 34 us -> 0 us
  matrix products: 19.2 us -> 0 us
    all_gather x2 -> x0, blocking collectives: 361 us -> none  [the longest x1 185 us: local(): lax.all_gather(own_rate, 'ctx', axis=1, tiled=True)]
    slice x34 -> x0, local copies, waits for them, and re-layouts: 150 us -> none  [the longest x2 77.4 us: shift_down(): lax.slice_in_dim(arr, 0, count - 1, axis=axis_b)]
    unnamed x130 -> x12, local copies, waits for them, and re-layouts: 104 us -> 5 us
    pad x36 -> x0, local copies, waits for them, and re-layouts: 90.5 us -> none  [the longest x24 88.6 us: prepare(): lax.associative_scan(partial(combine_fwd, lam_s), (spans, state_sum, mome...]
    all_to_all x4 -> x0, waiting for transfers between devices: 51.4 us -> none  [the longest x1 20.9 us: local(): lax.all_to_all(grad_gated_ch, 'ctx', split_axis=1, concat_axis=0, tiled=T...]
    pallas_call x0 -> x3, Pallas kernels: none -> 45.5 us  [the longest x1 33.8 us: local(): pl.pallas_call(exchange_kernel, out_shape=jax.ShapeDtypeStruct((INNER, 4...]
    all_to_all x4 -> x0, starting transfers between devices: 34 us -> none  [the longest x1 17 us: local(): lax.all_to_all(grad_t, 'ctx', split_axis=0, concat_axis=1, tiled=True)]
    add x54 -> x0, other arithmetic: 31.3 us -> none  [the longest x16 16 us: prepare(): lax.associative_scan(partial(combine_fwd, lam_s), (spans, state_sum, mome...]
  transfers between devices with their start and end apart: 4 -> 0, of which waited for: 3 -> 0; matrix products, arithmetic and copies ran while one was open for 2% -> 0% of each run, Pallas kernels for 0% -> 0%
where the time goes in v1:
time: 51.5 us; the launch traced here: 51.2 us
  Pallas kernels  45.5 us (88%)
  local copies, waits for them, and re-layouts  5 us (10%)
  between operations  0.68 us (1%)
    pallas_call x1, Pallas kernels, local(): pl.pallas_call(exchange_kernel, out_shape=jax.ShapeDtypeStruct((INNER, 4...  33.8 us
    pallas_call x1, Pallas kernels, local(): pl.pallas_call(finish_kernel, grid=(tiles,), out_shape=(jax.ShapeDtypeStr...  6.51 us
    pallas_call x1, Pallas kernels, local(): pl.pallas_call(state_kernel, grid=(tiles,), out_shape=(jax.ShapeDtypeStru...  5.18 us
    unnamed x12, local copies, waits for them, and re-layouts  5 us

profile of v1, /device:TPU:1, one launch (start us, length us, event | category | flops | bytes accessed | tf_op | source)
XLA Modules:
  0.0 51.2 jit_solution(1920635926864999841)
XLA Ops:
  0.6 0.0 copy-start
  0.6 1.0 %copy-done = bf16[256,1024]{1,0:T(8,128)(2,1)S(1)} copy-done((bf16[256,1024]{1,0:T(8,128)(2,1)S(1)}, bf16[256,1024]{1,0:T(8,128)(2,1)}, u32[]{:S(2)}) %copy-start) | copy-done | bytes 524312
  1.7 0.0 copy-start.1
  1.7 1.0 %copy-done.1 = bf16[256,1024]{1,0:T(8,128)(2,1)S(1)} copy-done((bf16[256,1024]{1,0:T(8,128)(2,1)S(1)}, bf16[256,1024]{1,0:T(8,128)(2,1)}, u32[]{:S(2)}) %copy-start.1) | copy-done | bytes 524312
  2.7 0.0 copy-start.2
  2.7 1.0 %copy-done.2 = bf16[256,1024]{1,0:T(8,128)(2,1)S(1)} copy-done((bf16[256,1024]{1,0:T(8,128)(2,1)S(1)}, bf16[256,1024]{1,0:T(8,128)(2,1)}, u32[]{:S(2)}) %copy-start.2) | copy-done | bytes 524312
  3.8 0.0 copy-start.3
  3.8 1.0 %copy-done.3 = bf16[256,1024]{1,0:T(8,128)(2,1)S(1)} copy-done((bf16[256,1024]{1,0:T(8,128)(2,1)S(1)}, bf16[256,1024]{1,0:T(8,128)(2,1)}, u32[]{:S(2)}) %copy-start.3) | copy-done | bytes 524312
  4.8 0.0 copy-start.4
  4.8 0.8 %copy-done.4 = f32[16,1024]{1,0:T(8,128)S(1)} copy-done((f32[16,1024]{1,0:T(8,128)S(1)}, f32[16,1024]{1,0:T(8,128)}, u32[]{:S(2)}) %copy-start.4) | copy-done | bytes 65560
  5.6 5.2 %states.1 = (bf16[16,16,1024]{2,1,0:T(8,128)(2,1)S(1)}, bf16[16,16,1024]{2,1,0:T(8,128)(2,1)S(1)}, bf16[8,96,128]{2,1,0:T(8,128)(2,1)S(1)}) custom-call(bf16[256,1024]{1,0:T(8,128)(2,1)S(1)} %copy-done, bf16[256,1024]{1,0:T(8,128)(2,1)S(1)} %copy-done.1, bf16[256,1024]{1,0:T(8,128)(2,1)S(1)} %copy-done.2, bf16[256,1024]{1,0:T(8,128)(2,1)S(1)} %copy-done.3, ...), custom_call_target="tpu_custom_call" | custom-call | tf_op jit(solution)/shard_map/states/pallas_call | solution.py:271
  10.8 0.0 copy-start.5
  10.8 33.8 %exchange.1.in_ref = bf16[8,64,128]{2,1,0:T(8,128)(2,1)S(1)} custom-call(bf16[8,96,128]{2,1,0:T(8,128)(2,1)S(1)} %get-tuple-element.10.send_a, f32[16,1024]{1,0:T(8,128)S(1)} %copy-done.4), custom_call_target="tpu_custom_call" | custom-call | tf_op jit(solution)/shard_map/exchange/pallas_call | solution.py:292
  44.6 0.0 copy-done.5
  44.7 6.5 %finish.1 = (bf16[256,1024]{1,0:T(8,128)(2,1)}, bf16[256,1024]{1,0:T(8,128)(2,1)}, bf16[256,1024]{1,0:T(8,128)(2,1)}, f32[16,1024]{1,0:T(8,128)}, f32[16,1024]{1,0:T(8,128)}) custom-call(bf16[256,1024]{1,0:T(8,128)(2,1)S(1)} %copy-done, bf16[256,1024]{1,0:T(8,128)(2,1)S(1)} %copy-done.1, bf16[256,1024]{1,0:T(8,128)(2,1)S(1)} %copy-done.2, ...), custom_call_target="tpu_custom_call" | custom-call | tf_op jit(solution)/shard_map/finish/pallas_call | solution.py:314
Async XLA Ops:
  0.6 1.0 %copy-start = (bf16[256,1024]{1,0:T(8,128)(2,1)S(1)}, bf16[256,1024]{1,0:T(8,128)(2,1)}, u32[]{:S(2)}) copy-start(bf16[256,1024]{1,0:T(8,128)(2,1)} %q_ref.3) | copy-start | bytes 1572868
  1.7 1.0 %copy-start.1 = (bf16[256,1024]{1,0:T(8,128)(2,1)S(1)}, bf16[256,1024]{1,0:T(8,128)(2,1)}, u32[]{:S(2)}) copy-start(bf16[256,1024]{1,0:T(8,128)(2,1)} %k_ref.3) | copy-start | bytes 1572868
  2.7 1.0 %copy-start.2 = (bf16[256,1024]{1,0:T(8,128)(2,1)S(1)}, bf16[256,1024]{1,0:T(8,128)(2,1)}, u32[]{:S(2)}) copy-start(bf16[256,1024]{1,0:T(8,128)(2,1)} %v_ref.3) | copy-start | bytes 1572868
  3.8 1.0 %copy-start.3 = (bf16[256,1024]{1,0:T(8,128)(2,1)S(1)}, bf16[256,1024]{1,0:T(8,128)(2,1)}, u32[]{:S(2)}) copy-start(bf16[256,1024]{1,0:T(8,128)(2,1)} %go_ref.3) | copy-start | bytes 1572868
  4.8 0.8 %copy-start.4 = (f32[16,1024]{1,0:T(8,128)S(1)}, f32[16,1024]{1,0:T(8,128)}, u32[]{:S(2)}) copy-start(f32[16,1024]{1,0:T(8,128)} %rate_ref.5) | copy-start | bytes 196612
  10.8 33.8 %copy-start.5 = (f32[16,1024]{1,0:T(8,128)S(1)}, f32[16,1024]{1,0:T(8,128)}, u32[]{:S(2)}) copy-start(f32[16,1024]{1,0:T(8,128)} %res_ref.1) | copy-start | bytes 196612

commit v2 on v1

v2 whole, which is shorter than its diff:
```python
import jax
import jax.numpy as jnp
from jax import lax
from jax.experimental import pallas as pl
from jax.experimental.pallas import tpu as pltpu
from jax.sharding import PartitionSpec as P

SEQ = 32768
MODES = 16
ROWS = 256
CHANS = 1024
SUB = 16
NSUB = ROWS // SUB
MID = 8
LANES = 128
TILE = 256
TILES = CHANS // TILE
HALVES = TILE // LANES
INNER = 8
OUTER = 16
VMEM_LIMIT = 63 * 2**20
F32 = jnp.float32
BF16 = jnp.bfloat16
MESH = pl.DeviceIdType.MESH


def iota(shape, dim):
    return lax.broadcasted_iota(jnp.int32, shape, dim)


def dot(a, b):
    return jnp.dot(a, b, preferred_element_type=F32)


def columns(t):
    return pl.ds(pl.multiple_of(t * TILE, TILE), TILE)


def spread(tab, val):
    return (tab * val[None]).reshape(tab.shape[0] * tab.shape[1], TILE)


def state_tables(t, rate, ptab, btab):
    cols = columns(t)
    pos = iota((SUB, TILE), 0).astype(F32)
    lam = rate[:, cols] * (1.0 / SEQ)
    for m in range(MODES):
        row = lam[m : m + 1, :]
        ptab[m, :, cols] = jnp.exp(-row * (SUB - 1.0 - pos)).astype(BF16)
        btab[m, :, cols] = jnp.exp(-row * (pos + 1.0)).astype(BF16)


def states(t, rate, u_ref, g_ref, ptab, btab, uf, gf, sub_s, sub_b, send_a):
    cols = columns(t)
    lam = rate[:, cols] * (1.0 / SEQ)
    out_row = iota((2 * MODES, MODES * SUB), 0)
    in_row = iota((2 * MODES, MODES * SUB), 1)
    hit = (in_row // SUB) == (out_row % MODES)
    off = (in_row % SUB).astype(F32)
    first = out_row < MODES
    sel_s = jnp.where(hit, jnp.where(first, 1.0, SUB - 1.0 - off), 0.0).astype(BF16)
    sel_b = jnp.where(hit, jnp.where(first, 1.0, off + 1.0), 0.0).astype(BF16)
    step = jnp.exp(-lam * SUB)
    zero = jnp.zeros((MODES, TILE), F32)
    s, q, bn, tn, gr, gw = zero, zero, zero, zero, zero, zero
    decay = jnp.ones((MODES, TILE), F32)
    for k in range(NSUB):
        rows = slice(k * SUB, (k + 1) * SUB)
        su = dot(sel_s, spread(ptab[:, :, cols], u_ref[rows, cols]))
        sg = dot(sel_b, spread(btab[:, :, cols], g_ref[rows, cols]))
        s_k, m_k = su[:MODES], su[MODES:]
        b_k, t_k = sg[:MODES], sg[MODES:]
        sub_s[k, :, cols] = s_k
        sub_b[k, :, cols] = b_k
        gr = gr + b_k * s
        gw = gw + t_k * s + b_k * q
        q = step * (q + float(SUB) * s) + m_k
        s = step * s + s_k
        db = decay * b_k
        bn = bn + db
        tn = tn + decay * t_k + float(k * SUB) * db
        decay = decay * step
    halves = []
    for half in range(HALVES):
        acc = [jnp.zeros((8, LANES), F32) for _ in range(SUB)]
        for octet in range(NSUB // 8):
            us = [uf[half, pl.ds(octet * 8 * SUB + b, 8, stride=SUB), :] for b in range(SUB)]
            for b in range(SUB):
                gb = gf[half, pl.ds(octet * 8 * SUB + b, 8, stride=SUB), :]
                for lag in range(b + 1):
                    acc[lag] = acc[lag] + gb * us[b - lag]
        halves.append([jnp.sum(a, axis=0, keepdims=True) for a in acc])
    unit = jnp.exp(-lam)
    power = jnp.ones((MODES, TILE), F32)
    for lag in range(SUB):
        term = jnp.concatenate([h[lag] for h in halves], axis=1) * power
        gr = gr + term
        gw = gw + float(lag) * term
        power = power * unit
    for half in range(HALVES):
        part_cols = slice(half * LANES, (half + 1) * LANES)
        for n, part in enumerate((s, q, bn, tn, gr, gw)):
            send_a[t * HALVES + half, n * MODES : (n + 1) * MODES, :] = part[:, part_cols].astype(BF16)


def near_part(t, rate, res, u_ref, g_ref, wtab, vtab, htab, near_c, near_g):
    cols = columns(t)
    lam = rate[:, cols] * (1.0 / SEQ)
    unit = jnp.exp(-lam)
    power = res[:, cols]
    mid = power * jnp.exp(-lam * float(MID))
    for b in range(SUB):
        htab[b] = jnp.broadcast_to(jnp.sum(power, axis=0, keepdims=True), (SUB, TILE)).astype(BF16)
        vtab[SUB - 1 - b, :, cols] = (power - mid).astype(BF16)
        power = power * unit
        wtab[b, :, cols] = (power - mid).astype(BF16)
    out_row = iota((SUB, SUB * SUB), 0)
    in_row = iota((SUB, SUB * SUB), 1)
    lag, pos = in_row // SUB, in_row % SUB
    down = jnp.where(pos + lag == out_row, 1.0, 0.0).astype(BF16)
    up = jnp.where(pos - lag == out_row, 1.0, 0.0).astype(BF16)
    for k in range(NSUB):
        rows = slice(k * SUB, (k + 1) * SUB)
        near_c[rows, cols] = dot(down, spread(htab[...], u_ref[rows, cols]))
        near_g[rows, cols] = dot(up, spread(htab[...], g_ref[rows, cols]))


def far_part(t, rate, res, k_in, v_in, go_in, wtab, vtab, sub_s, sub_b, near_c, near_g, recv_c, gq, gk, gv):
    cols = columns(t)
    lam = rate[:, cols] * (1.0 / SEQ)
    step = jnp.exp(-lam * SUB)
    mid = res[:, cols] * jnp.exp(-lam * float(MID))

    def incoming(n):
        parts = [recv_c[t * HALVES + h, n * MODES : (n + 1) * MODES, :] for h in range(HALVES)]
        return jnp.concatenate(parts, axis=1)

    out_row = iota((SUB, SUB * MODES), 0)
    in_row = iota((SUB, SUB * MODES), 1)
    pick = jnp.where(in_row // MODES == out_row, 1.0, 0.0).astype(BF16)

    def reach(tab, x):
        base = jnp.sum(mid * x, axis=0, keepdims=True)
        return dot(pick, spread(tab[:, :, cols], x.astype(BF16))) + base

    x = incoming(0)
    for k in range(NSUB):
        rows = slice(k * SUB, (k + 1) * SUB)
        conv = near_c[rows, cols] + reach(wtab, x)
        gq[rows, cols] = (go_in[rows, cols].astype(F32) * conv).astype(BF16)
        x = step * x + sub_s[k, :, cols]
    x = incoming(1)
    for k in reversed(range(NSUB)):
        rows = slice(k * SUB, (k + 1) * SUB)
        grad = near_g[rows, cols] + reach(vtab, x)
        gk[rows, cols] = (v_in[rows, cols].astype(F32) * grad).astype(BF16)
        gv[rows, cols] = (k_in[rows, cols].astype(F32) * grad).astype(BF16)
        x = step * x + sub_b[k, :, cols]


def main_kernel(
    q_hbm, k_hbm, v_hbm, go_hbm, res_hbm, rate_hbm,
    gq_hbm, gk_hbm, gv_hbm, gres_hbm, grate_hbm,
    gq, gk, gv, gres, grate, q_in, k_in, v_in, go_in, res, rate, u_ref, g_ref, uf, gf, ptab, btab, wtab, vtab, htab,
    sub_s, sub_b, near_c, near_g,
    send_a, recv_a, pre_s, pre_b, send_b, recv_b, send_m, recv_m, send_d, recv_d, send_c, recv_c, send_e, recv_e,
    in_sem, par_sem, out_sem, sa, ra, sb, rb, sm, rm, sd, rd, sc, rc, se, re,
):
    me = lax.axis_index("ctx")
    grp = me // INNER
    idx = me % INNER
    inner = [(idx + d) % INNER for d in (4, 5, 3, 2, 6, 7, 1)]
    outer = [(grp + d) % OUTER for d in (12, 4, 11, 13, 5, 3, 10, 6, 14, 2, 9, 7, 8, 15, 1)]

    def to_inner(j):
        return {"ctx": grp * INNER + j}

    def to_outer(p):
        return {"ctx": p * INNER + idx}

    pairs = ((q_hbm, q_in), (k_hbm, k_in), (v_hbm, v_in), (go_hbm, go_in))

    def load(t, n):
        src, dst = pairs[n]
        return pltpu.make_async_copy(src.at[:, columns(t)], dst.at[:, columns(t)], in_sem.at[t, n])

    params = (
        pltpu.make_async_copy(rate_hbm, rate, par_sem.at[0]),
        pltpu.make_async_copy(res_hbm, res, par_sem.at[1]),
    )
    for cp in params:
        cp.start()
    for t in range(TILES):
        for n in range(4):
            load(t, n).start()

    barrier = pltpu.get_barrier_semaphore()
    for j in inner:
        pl.semaphore_signal(barrier, inc=1, device_id=to_inner(j), device_id_type=MESH)
    for p in outer:
        pl.semaphore_signal(barrier, inc=1, device_id=to_outer(p), device_id_type=MESH)

    def remote(src, dst, ssem, rsem, target):
        return pltpu.make_async_remote_copy(
            src_ref=src, dst_ref=dst, send_sem=ssem, recv_sem=rsem, device_id=target, device_id_type=MESH
        )

    for cp in params:
        cp.wait()

    @pl.loop(0, TILES)
    def _(t):
        state_tables(t, rate, ptab, btab)

    @pl.loop(0, TILES)
    def _(t):
        cols = columns(t)
        for n in range(4):
            load(t, n).wait()
        u = (k_in[:, cols].astype(F32) * v_in[:, cols].astype(F32)).astype(BF16)
        g = (go_in[:, cols].astype(F32) * q_in[:, cols].astype(F32)).astype(BF16)
        u_ref[:, cols] = u
        g_ref[:, cols] = g
        for half in range(HALVES):
            part = slice(half * LANES, (half + 1) * LANES)
            uf[half] = u[:, part].astype(F32)
            gf[half] = g[:, part].astype(F32)
        states(t, rate, u_ref, g_ref, ptab, btab, uf, gf, sub_s, sub_b, send_a)

    pl.semaphore_wait(barrier, INNER + OUTER - 2)

    for j in inner:
        remote(send_a.at[j], recv_a.at[idx], sa.at[j], ra.at[idx], to_inner(j)).start()
    recv_a[idx] = send_a[idx]

    @pl.loop(0, TILES)
    def _(t):
        near_part(t, rate, res, u_ref, g_ref, wtab, vtab, htab, near_c, near_g)

    block = pl.ds(pl.multiple_of(idx * LANES, LANES), LANES)
    lam = rate[:, block] * (1.0 / SEQ)
    dec = jnp.exp(-lam * float(ROWS))
    span = float(ROWS * INNER)
    dec_g = jnp.exp(-lam * span)
    for j in inner:
        remote(send_a.at[j], recv_a.at[j], sa.at[j], ra.at[j], to_inner(j)).wait_recv()
    zero = jnp.zeros((MODES, LANES), F32)
    s, q, gr, gw, bn, tn = zero, zero, zero, zero, zero, zero
    front = jnp.ones((MODES, LANES), F32)
    nears = []
    for j in range(INNER):
        part = [recv_a[j, n * MODES : (n + 1) * MODES, :].astype(F32) for n in range(6)]
        s_j, m_j, b_j, t_j, gr_j, gw_j = part
        pre_s[j] = s
        nears.append(b_j)
        gr = gr + gr_j + b_j * s
        gw = gw + gw_j + t_j * s + b_j * q
        q = dec * (q + float(ROWS) * s) + m_j
        s = dec * s + s_j
        db = front * b_j
        bn = bn + db
        tn = tn + front * t_j + float(ROWS * j) * db
        front = front * dec
    for n, part in enumerate((s, q, bn, tn, gr, gw)):
        send_b[:, n, :] = part
    send_m[0] = bn
    send_m[1] = s

    for p in outer:
        remote(send_b.at[p], recv_b.at[grp], sb.at[p], rb.at[grp], to_outer(p)).start()
    for p in outer:
        pick = (p > grp).astype(jnp.int32)
        remote(send_m.at[pick], recv_m.at[grp], sm.at[p], rm.at[grp], to_outer(p)).start()
    recv_b[grp] = send_b[grp]
    recv_m[grp] = zero
    back = zero
    for j in reversed(range(INNER)):
        pre_b[j] = back
        back = dec * back + nears[j]
    decs = [jnp.ones((MODES, LANES), F32)]
    for j in range(1, INNER):
        decs.append(decs[-1] * dec)
    mine = iota((MODES, LANES), 0) == grp
    lam_row = jnp.sum(jnp.where(mine, lam, 0.0), axis=0, keepdims=True)
    dec_row = jnp.exp(-lam_row * span)

    for p in outer:
        remote(send_b.at[p], recv_b.at[p], sb.at[p], rb.at[p], to_outer(p)).wait_recv()
    zrow = jnp.zeros((1, LANES), F32)
    s, q, gr, gw = zrow, zrow, zrow, zrow
    for p in range(OUTER):
        s_p, m_p, b_p, t_p, gr_p, gw_p = [recv_b[p, n : n + 1, :] for n in range(6)]
        gr = gr + gr_p + b_p * s
        gw = gw + gw_p + t_p * s + b_p * q
        q = dec_row * (q + span * s) + m_p
        s = dec_row * s + s_p
    send_d[0:1, :] = gr
    send_d[1:2, :] = gw
    for p in outer:
        remote(send_d, recv_d.at[grp], sd.at[p], rd.at[grp], to_outer(p)).start()
    recv_d[grp] = send_d[...]

    for p in outer:
        remote(send_m.at[0], recv_m.at[p], sm.at[p], rm.at[p], to_outer(p)).wait_recv()
    state, back = zero, zero
    for p in range(OUTER):
        state = jnp.where(p < grp, dec_g * state + recv_m[p], state)
    for p in reversed(range(OUTER)):
        back = jnp.where(p > grp, dec_g * back + recv_m[p], back)

    for j in range(INNER):
        send_c[j, 0:MODES, :] = pre_s[j] + decs[j] * state
        send_c[j, MODES : 2 * MODES, :] = pre_b[j] + decs[INNER - 1 - j] * back
    for j in inner:
        remote(send_c.at[j], recv_c.at[idx], sc.at[j], rc.at[idx], to_inner(j)).start()
    recv_c[idx] = send_c[idx]

    for p in outer:
        remote(send_d, recv_d.at[p], sd.at[p], rd.at[p], to_outer(p)).wait_recv()
    send_e[0:MODES, :] = recv_d[:, 0, :].astype(BF16)
    send_e[MODES : 2 * MODES, :] = recv_d[:, 1, :].astype(BF16)
    for j in inner:
        remote(send_e, recv_e.at[idx], se.at[j], re.at[idx], to_inner(j)).start()
    recv_e[idx] = send_e[...]

    for j in inner:
        remote(send_c.at[j], recv_c.at[j], sc.at[j], rc.at[j], to_inner(j)).wait_recv()

    results = ((gq, gq_hbm), (gk, gk_hbm), (gv, gv_hbm))

    def store(t, n):
        src, dst = results[n]
        return pltpu.make_async_copy(src.at[:, columns(t)], dst.at[:, columns(t)], out_sem.at[t, n])

    @pl.loop(0, TILES)
    def _(t):
        far_part(t, rate, res, k_in, v_in, go_in, wtab, vtab, sub_s, sub_b, near_c, near_g, recv_c, gq, gk, gv)
        for n in range(3):
            store(t, n).start()

    for j in inner:
        remote(send_e, recv_e.at[j], se.at[j], re.at[j], to_inner(j)).wait_recv()
    scale = SEQ ** -0.5
    for j in range(INNER):
        cols = slice(j * LANES, (j + 1) * LANES)
        gres[:, cols] = scale * recv_e[j, 0:MODES, :].astype(F32)
        grate[:, cols] = (-scale / SEQ) * res[:, cols] * recv_e[j, MODES : 2 * MODES, :].astype(F32)

    sums = (
        pltpu.make_async_copy(gres, gres_hbm, par_sem.at[0]),
        pltpu.make_async_copy(grate, grate_hbm, par_sem.at[1]),
    )
    for cp in sums:
        cp.start()
    for j in inner:
        remote(send_a.at[j], recv_a.at[j], sa.at[j], ra.at[j], to_inner(j)).wait_send()
        remote(send_c.at[j], recv_c.at[j], sc.at[j], rc.at[j], to_inner(j)).wait_send()
        remote(send_e, recv_e.at[j], se.at[j], re.at[j], to_inner(j)).wait_send()
    for p in outer:
        remote(send_b.at[p], recv_b.at[p], sb.at[p], rb.at[p], to_outer(p)).wait_send()
        remote(send_m.at[0], recv_m.at[p], sm.at[p], rm.at[p], to_outer(p)).wait_send()
        remote(send_d, recv_d.at[p], sd.at[p], rd.at[p], to_outer(p)).wait_send()
    for t in range(TILES):
        for n in range(3):
            store(t, n).wait()
    for cp in sums:
        cp.wait()


def store_kernel(*refs):
    srcs, dsts, sem = refs[:5], refs[5:10], refs[10]
    copies = [pltpu.make_async_copy(s, d, sem.at[n]) for n, (s, d) in enumerate(zip(srcs, dsts))]
    for cp in copies:
        cp.start()
    for cp in copies:
        cp.wait()


def local(query, key_in, value, grad_out, residue, rate):
    hbm = pl.BlockSpec(memory_space=pltpu.HBM)
    big = jax.ShapeDtypeStruct((ROWS, CHANS), BF16)
    small = jax.ShapeDtypeStruct((MODES, CHANS), F32)
    dma = pltpu.SemaphoreType.DMA

    def buf(*shape, dtype=F32):
        return pltpu.VMEM(shape, dtype)

    results = pl.pallas_call(
        main_kernel,
        out_shape=(big, big, big, small, small),
        in_specs=[hbm] * 6,
        out_specs=[hbm] * 5,
        scratch_shapes=[
            *[buf(ROWS, CHANS, dtype=BF16)] * 3,
            *[buf(MODES, CHANS)] * 2,
            *[buf(ROWS, CHANS, dtype=BF16)] * 4,
            *[buf(MODES, CHANS)] * 2,
            *[buf(ROWS, CHANS, dtype=BF16)] * 2,
            *[buf(HALVES, ROWS, LANES)] * 2,
            *[buf(MODES, SUB, CHANS, dtype=BF16)] * 2,
            *[buf(SUB, MODES, CHANS, dtype=BF16)] * 2,
            buf(SUB, SUB, TILE, dtype=BF16),
            *[buf(NSUB, MODES, CHANS)] * 2,
            *[buf(ROWS, CHANS)] * 2,
            *[buf(INNER, 6 * MODES, LANES, dtype=BF16)] * 2,
            *[buf(INNER, MODES, LANES)] * 2,
            *[buf(OUTER, 8, LANES)] * 2,
            buf(2, MODES, LANES), buf(OUTER, MODES, LANES),
            buf(8, LANES), buf(OUTER, 8, LANES),
            *[buf(INNER, 2 * MODES, LANES)] * 2,
            buf(2 * MODES, LANES, dtype=BF16), buf(INNER, 2 * MODES, LANES, dtype=BF16),
            dma((TILES, 4)), dma((2,)), dma((TILES, 3)),
            dma((INNER,)), dma((INNER,)), dma((OUTER,)), dma((OUTER,)), dma((OUTER,)), dma((OUTER,)),
            dma((OUTER,)), dma((OUTER,)), dma((INNER,)), dma((INNER,)), dma((INNER,)), dma((INNER,)),
        ],
        compiler_params=pltpu.CompilerParams(collective_id=0, has_side_effects=True, vmem_limit_bytes=VMEM_LIMIT),
        name="hyena",
    )(query, key_in, value, grad_out, residue, rate)

    return pl.pallas_call(
        store_kernel,
        out_shape=(big, big, big, small, small),
        in_specs=[hbm] * 5,
        out_specs=[hbm] * 5,
        scratch_shapes=[dma((5,))],
        compiler_params=pltpu.CompilerParams(vmem_limit_bytes=VMEM_LIMIT),
        name="store",
    )(*results)


def solution(mesh):
    big, small = P("ctx", "tp"), P(None, "tp")
    return jax.shard_map(
        local, mesh=mesh, in_specs=(big, big, big, big, small, small),
        out_specs=(big, big, big, small, small), check_vma=False,
    )
```

time: 51.5 us -> 90.5 us (1.76)
  Pallas kernels: 45.5 us -> 89.7 us
  local copies, waits for them, and re-layouts: 5 us -> 0 us
    pallas_call x3 -> x2, Pallas kernels: 45.5 us -> 89.7 us  [the longest x1 52.8 us: local(): pl.pallas_call(store_kernel, out_shape=(big, big, big, small, small), in_...]
    unnamed x12 -> x0, local copies, waits for them, and re-layouts: 5 us -> none
where the time goes in v2:
time: 90.5 us; the launch traced here: 90.4 us
  Pallas kernels  89.7 us (99%)
    pallas_call x1, Pallas kernels, local(): pl.pallas_call(store_kernel, out_shape=(big, big, big, small, small), in_...  52.8 us
    pallas_call x1, Pallas kernels, local(): pl.pallas_call(main_kernel, out_shape=(big, big, big, small, small), in_s...  37 us

profile of v2, /device:TPU:1, one launch (start us, length us, event | category | flops | bytes accessed | tf_op | source)
XLA Modules:
  0.0 90.4 jit_solution(13319896539081593816)
XLA Ops:
  0.6 37.0 %hyena.1 = (bf16[256,1024]{1,0:T(8,128)(2,1)}, bf16[256,1024]{1,0:T(8,128)(2,1)}, bf16[256,1024]{1,0:T(8,128)(2,1)}, f32[16,1024]{1,0:T(8,128)}, f32[16,1024]{1,0:T(8,128)}) custom-call(bf16[256,1024]{1,0:T(8,128)(2,1)} %q_hbm.1, bf16[256,1024]{1,0:T(8,128)(2,1)} %k_hbm.1, bf16[256,1024]{1,0:T(8,128)(2,1)} %v_hbm.1, bf16[256,1024]{1,0:T(8,128)(2,1)} %go_hbm.1, ...), custom_call_target="tpu_custom_call" | custom-call | tf_op jit(solution)/shard_map/hyena/pallas_call | solution.py:388
  37.6 52.8 %store.1 = (bf16[256,1024]{1,0:T(8,128)(2,1)}, bf16[256,1024]{1,0:T(8,128)(2,1)}, bf16[256,1024]{1,0:T(8,128)(2,1)}, f32[16,1024]{1,0:T(8,128)}, f32[16,1024]{1,0:T(8,128)}) custom-call(bf16[256,1024]{1,0:T(8,128)(2,1)} %get-tuple-element.10.refs_0_, bf16[256,1024]{1,0:T(8,128)(2,1)} %get-tuple-element.11.refs_1_, ...), custom_call_target="tpu_custom_call" | custom-call | tf_op jit(solution)/shard_map/store/pallas_call | solution.py:420

commit v3 on v2

--- a/solution.py
+++ b/solution.py
@@ -368,11 +368,15 @@
 
 
 def store_kernel(*refs):
-    srcs, dsts, sem = refs[:5], refs[5:10], refs[10]
-    copies = [pltpu.make_async_copy(s, d, sem.at[n]) for n, (s, d) in enumerate(zip(srcs, dsts))]
-    for cp in copies:
+    srcs, dsts, held, sem_in, sem_out = refs[:5], refs[5:10], refs[10:15], refs[15], refs[16]
+    loads = [pltpu.make_async_copy(s, h, sem_in.at[n]) for n, (s, h) in enumerate(zip(srcs, held))]
+    stores = [pltpu.make_async_copy(h, d, sem_out.at[n]) for n, (h, d) in enumerate(zip(held, dsts))]
+    for cp in loads:
         cp.start()
-    for cp in copies:
+    for load, store in zip(loads, stores):
+        load.wait()
+        store.start()
+    for cp in stores:
         cp.wait()
 
 
@@ -422,7 +426,12 @@
         out_shape=(big, big, big, small, small),
         in_specs=[hbm] * 5,
         out_specs=[hbm] * 5,
-        scratch_shapes=[dma((5,))],
+        scratch_shapes=[
+            *[buf(ROWS, CHANS, dtype=BF16)] * 3,
+            *[buf(MODES, CHANS)] * 2,
+            dma((5,)),
+            dma((5,)),
+        ],
         compiler_params=pltpu.CompilerParams(vmem_limit_bytes=VMEM_LIMIT),
         name="store",
     )(*results)

time: 90.5 us -> 40 us (0.44)
  Pallas kernels: 89.7 us -> 39.3 us
    pallas_call x1, Pallas kernels: 52.8 us -> 2.3 us  [local(): pl.pallas_call(store_kernel, out_shape=(big, big, big, small, small), in_...]
where the time goes in v3:
time: 40 us; the launch traced here: 39.9 us
  Pallas kernels  39.3 us (98%)
  between operations  0.64 us (2%)
    pallas_call x1, Pallas kernels, local(): pl.pallas_call(main_kernel, out_shape=(big, big, big, small, small), in_s...  37 us
    pallas_call x1, Pallas kernels, local(): pl.pallas_call(store_kernel, out_shape=(big, big, big, small, small), in_...  2.3 us

profile of v3, /device:TPU:1, one launch (start us, length us, event | category | flops | bytes accessed | tf_op | source)
XLA Modules:
  0.0 39.9 jit_solution(10842280536127902529)
XLA Ops:
  0.6 37.0 %hyena.1 = (bf16[256,1024]{1,0:T(8,128)(2,1)}, bf16[256,1024]{1,0:T(8,128)(2,1)}, bf16[256,1024]{1,0:T(8,128)(2,1)}, f32[16,1024]{1,0:T(8,128)}, f32[16,1024]{1,0:T(8,128)}) custom-call(bf16[256,1024]{1,0:T(8,128)(2,1)} %q_hbm.1, bf16[256,1024]{1,0:T(8,128)(2,1)} %k_hbm.1, bf16[256,1024]{1,0:T(8,128)(2,1)} %v_hbm.1, bf16[256,1024]{1,0:T(8,128)(2,1)} %go_hbm.1, ...), custom_call_target="tpu_custom_call" | custom-call | tf_op jit(solution)/shard_map/hyena/pallas_call | solution.py:392
  37.6 2.3 %store.1 = (bf16[256,1024]{1,0:T(8,128)(2,1)}, bf16[256,1024]{1,0:T(8,128)(2,1)}, bf16[256,1024]{1,0:T(8,128)(2,1)}, f32[16,1024]{1,0:T(8,128)}, f32[16,1024]{1,0:T(8,128)}) custom-call(bf16[256,1024]{1,0:T(8,128)(2,1)} %get-tuple-element.10.refs_0_, bf16[256,1024]{1,0:T(8,128)(2,1)} %get-tuple-element.11.refs_1_, ...), custom_call_target="tpu_custom_call" | custom-call | tf_op jit(solution)/shard_map/store/pallas_call | solution.py:424

commit v4 on v3

v4 whole, which is shorter than its diff:
```python
import jax
import jax.numpy as jnp
from jax import lax
from jax.experimental import pallas as pl
from jax.experimental.pallas import tpu as pltpu
from jax.sharding import PartitionSpec as P

SEQ = 32768
MODES = 16
ROWS = 256
CHANS = 1024
SUB = 16
NSUB = ROWS // SUB
MID = 8
LANES = 128
TILE = 256
TILES = CHANS // TILE
HALVES = TILE // LANES
RUN = 8
SEGS = 2
DEPTH = 8
GROUP = SEGS * RUN
HALF = MODES // SEGS
VMEM_LIMIT = 63 * 2**20
F32 = jnp.float32
BF16 = jnp.bfloat16
MESH = pl.DeviceIdType.MESH


def iota(shape, dim):
    return lax.broadcasted_iota(jnp.int32, shape, dim)


def dot(a, b):
    return jnp.dot(a, b, preferred_element_type=F32)


def columns(t):
    return pl.ds(pl.multiple_of(t * TILE, TILE), TILE)


def spread(tab, val):
    return (tab * val[None]).reshape(tab.shape[0] * tab.shape[1], TILE)


def state_tables(t, rate, ptab, btab):
    cols = columns(t)
    pos = iota((SUB, TILE), 0).astype(F32)
    lam = rate[:, cols] * (1.0 / SEQ)
    for m in range(MODES):
        row = lam[m : m + 1, :]
        ptab[m, :, cols] = jnp.exp(-row * (SUB - 1.0 - pos)).astype(BF16)
        btab[m, :, cols] = jnp.exp(-row * (pos + 1.0)).astype(BF16)


def states(t, rate, u_ref, g_ref, ptab, btab, uf, gf, sub_s, sub_b, send_a):
    cols = columns(t)
    lam = rate[:, cols] * (1.0 / SEQ)
    out_row = iota((2 * MODES, MODES * SUB), 0)
    in_row = iota((2 * MODES, MODES * SUB), 1)
    hit = (in_row // SUB) == (out_row % MODES)
    off = (in_row % SUB).astype(F32)
    first = out_row < MODES
    sel_s = jnp.where(hit, jnp.where(first, 1.0, SUB - 1.0 - off), 0.0).astype(BF16)
    sel_b = jnp.where(hit, jnp.where(first, 1.0, off + 1.0), 0.0).astype(BF16)
    step = jnp.exp(-lam * SUB)
    zero = jnp.zeros((MODES, TILE), F32)
    s, q, bn, tn, gr, gw = zero, zero, zero, zero, zero, zero
    decay = jnp.ones((MODES, TILE), F32)
    for k in range(NSUB):
        rows = slice(k * SUB, (k + 1) * SUB)
        su = dot(sel_s, spread(ptab[:, :, cols], u_ref[rows, cols]))
        sg = dot(sel_b, spread(btab[:, :, cols], g_ref[rows, cols]))
        s_k, m_k = su[:MODES], su[MODES:]
        b_k, t_k = sg[:MODES], sg[MODES:]
        sub_s[k, :, cols] = s_k
        sub_b[k, :, cols] = b_k
        gr = gr + b_k * s
        gw = gw + t_k * s + b_k * q
        q = step * (q + float(SUB) * s) + m_k
        s = step * s + s_k
        db = decay * b_k
        bn = bn + db
        tn = tn + decay * t_k + float(k * SUB) * db
        decay = decay * step
    halves = []
    for half in range(HALVES):
        acc = [jnp.zeros((8, LANES), F32) for _ in range(SUB)]
        for octet in range(NSUB // 8):
            us = [uf[half, pl.ds(octet * 8 * SUB + b, 8, stride=SUB), :] for b in range(SUB)]
            for b in range(SUB):
                gb = gf[half, pl.ds(octet * 8 * SUB + b, 8, stride=SUB), :]
                for lag in range(b + 1):
                    acc[lag] = acc[lag] + gb * us[b - lag]
        halves.append([jnp.sum(a, axis=0, keepdims=True) for a in acc])
    unit = jnp.exp(-lam)
    power = jnp.ones((MODES, TILE), F32)
    for lag in range(SUB):
        term = jnp.concatenate([h[lag] for h in halves], axis=1) * power
        gr = gr + term
        gw = gw + float(lag) * term
        power = power * unit
    for half in range(HALVES):
        part_cols = slice(half * LANES, (half + 1) * LANES)
        for x in range(SEGS):
            modes = slice(x * HALF, (x + 1) * HALF)
            parts = [part[modes, part_cols] for part in (s, q, bn, tn, gr, gw)]
            send_a[x * RUN + t * HALVES + half] = jnp.concatenate(parts, axis=0).astype(BF16)


def near_part(t, rate, res, u_ref, g_ref, wtab, vtab, htab, near_c, near_g):
    cols = columns(t)
    lam = rate[:, cols] * (1.0 / SEQ)
    unit = jnp.exp(-lam)
    power = res[:, cols]
    mid = power * jnp.exp(-lam * float(MID))
    powers = []
    for b in range(SUB):
        htab[b] = jnp.broadcast_to(jnp.sum(power, axis=0, keepdims=True), (SUB, TILE)).astype(BF16)
        powers.append(power - mid)
        power = power * unit
    powers.append(power - mid)
    for i in range(SUB // 2):
        for h in range(2):
            modes = slice(h * HALF, (h + 1) * HALF)
            pair = (powers[2 * i + 1][modes], powers[2 * i + 2][modes])
            wtab[h, i, :, cols] = jnp.concatenate(pair, axis=0).astype(BF16)
            pair = (powers[SUB - 1 - 2 * i][modes], powers[SUB - 2 - 2 * i][modes])
            vtab[h, i, :, cols] = jnp.concatenate(pair, axis=0).astype(BF16)
    out_row = iota((SUB, SUB * SUB), 0)
    in_row = iota((SUB, SUB * SUB), 1)
    lag, pos = in_row // SUB, in_row % SUB
    down = jnp.where(pos + lag == out_row, 1.0, 0.0).astype(BF16)
    up = jnp.where(pos - lag == out_row, 1.0, 0.0).astype(BF16)
    for k in range(NSUB):
        rows = slice(k * SUB, (k + 1) * SUB)
        near_c[rows, cols] = dot(down, spread(htab[...], u_ref[rows, cols]))
        near_g[rows, cols] = dot(up, spread(htab[...], g_ref[rows, cols]))


def far_part(t, rate, res, k_in, v_in, go_in, wtab, vtab, sub_s, sub_b, near_c, near_g, recv_c, gq, gk, gv):
    cols = columns(t)
    lam = rate[:, cols] * (1.0 / SEQ)
    step = jnp.exp(-lam * SUB)
    mid = res[:, cols] * jnp.exp(-lam * float(MID))

    def incoming(n):
        rows = slice(n * HALF, (n + 1) * HALF)
        parts = [
            jnp.concatenate([recv_c[x * RUN + t * HALVES + h, rows, :] for x in range(SEGS)], axis=0)
            for h in range(HALVES)
        ]
        return jnp.concatenate(parts, axis=1)

    out_row = iota((2 * SUB, SUB * MODES), 0)
    in_row = iota((2 * SUB, SUB * MODES), 1)
    pick = jnp.where(in_row // HALF == out_row, 1.0, 0.0).astype(BF16)

    def reach(tab, xs):
        sums = []
        bases = []
        for x in xs:
            bases.append(jnp.broadcast_to(jnp.sum(mid * x, axis=0, keepdims=True), (SUB, TILE)))
            low = jnp.concatenate([x[:HALF], x[:HALF]], axis=0).astype(BF16)
            high = jnp.concatenate([x[HALF:], x[HALF:]], axis=0).astype(BF16)
            sums.append((tab[0, :, :, cols] * low[None] + tab[1, :, :, cols] * high[None]).reshape(SUB * HALF, TILE))
        return dot(pick, jnp.concatenate(sums, axis=0)) + jnp.concatenate(bases, axis=0)

    x = incoming(0)
    for k in range(0, NSUB, 2):
        rows = slice(k * SUB, (k + 2) * SUB)
        after = step * x + sub_s[k, :, cols]
        conv = near_c[rows, cols] + reach(wtab, (x, after))
        gq[rows, cols] = (go_in[rows, cols].astype(F32) * conv).astype(BF16)
        x = step * after + sub_s[k + 1, :, cols]
    x = incoming(1)
    for k in reversed(range(0, NSUB, 2)):
        rows = slice(k * SUB, (k + 2) * SUB)
        before = step * x + sub_b[k + 1, :, cols]
        grad = near_g[rows, cols] + reach(vtab, (before, x))
        gk[rows, cols] = (v_in[rows, cols].astype(F32) * grad).astype(BF16)
        gv[rows, cols] = (k_in[rows, cols].astype(F32) * grad).astype(BF16)
        x = step * before + sub_b[k, :, cols]


def main_kernel(
    q_hbm, k_hbm, v_hbm, go_hbm, res_hbm, rate_hbm,
    gq_hbm, gk_hbm, gv_hbm, gres_hbm, grate_hbm,
    gq, gk, gv, gres, grate, q_in, k_in, v_in, go_in, res, rate, u_ref, g_ref, uf, gf, ptab, btab, wtab, vtab, htab,
    sub_s, sub_b, near_c, near_g,
    send_a, recv_a, pre_s, pre_b, send_m, recv_m, send_x, recv_x, send_c, recv_c, send_e, recv_e,
    in_sem, par_sem, out_sem, sa, ra, sm, rm, sx, rx, sc, rc, se, re,
):
    me = lax.axis_index("ctx")
    seg = me // (DEPTH * RUN)
    z = (me // RUN) % DEPTH
    y = (me % RUN) // 2
    own = seg * RUN + me % RUN
    others = [(own + d) % GROUP for d in (12, 4, 11, 5, 13, 3, 10, 6, 14, 2, 9, 7, 8, 15, 1)]
    layers = [(z + d) % DEPTH for d in (4, 5, 3, 6, 2, 7, 1)]

    def member(j):
        return {"ctx": (j // RUN) * (DEPTH * RUN) + z * RUN + j % RUN}

    def layer(p):
        return {"ctx": seg * (DEPTH * RUN) + p * RUN + me % RUN}

    def gray(n):
        return n + n // 2 - 2 * (n // 3)

    def tile_at(n):
        return (y + gray(n)) % TILES

    pairs = ((q_hbm, q_in), (k_hbm, k_in), (v_hbm, v_in), (go_hbm, go_in))

    def load(t, n):
        src, dst = pairs[n]
        return pltpu.make_async_copy(src.at[:, columns(t)], dst.at[:, columns(t)], in_sem.at[t, n])

    params = (
        pltpu.make_async_copy(rate_hbm, rate, par_sem.at[0]),
        pltpu.make_async_copy(res_hbm, res, par_sem.at[1]),
    )
    for cp in params:
        cp.start()
    for n in reversed(range(TILES)):
        for i in range(4):
            load(tile_at(n), i).start()

    barrier = pltpu.get_barrier_semaphore()
    for j in others:
        pl.semaphore_signal(barrier, inc=1, device_id=member(j), device_id_type=MESH)
    for p in layers:
        pl.semaphore_signal(barrier, inc=1, device_id=layer(p), device_id_type=MESH)

    def remote(src, dst, ssem, rsem, target):
        return pltpu.make_async_remote_copy(
            src_ref=src, dst_ref=dst, send_sem=ssem, recv_sem=rsem, device_id=target, device_id_type=MESH
        )

    for cp in params:
        cp.wait()

    @pl.loop(0, TILES)
    def _(t):
        state_tables(t, rate, ptab, btab)

    def tile_states(t):
        cols = columns(t)
        for n in range(4):
            load(t, n).wait()
        u = (k_in[:, cols].astype(F32) * v_in[:, cols].astype(F32)).astype(BF16)
        g = (go_in[:, cols].astype(F32) * q_in[:, cols].astype(F32)).astype(BF16)
        u_ref[:, cols] = u
        g_ref[:, cols] = g
        for half in range(HALVES):
            part = slice(half * LANES, (half + 1) * LANES)
            uf[half] = u[:, part].astype(F32)
            gf[half] = g[:, part].astype(F32)
        states(t, rate, u_ref, g_ref, ptab, btab, uf, gf, sub_s, sub_b, send_a)

    def tile_owners(t):
        return [x * RUN + t * HALVES + half for x in range(SEGS) for half in range(HALVES)]

    def tile_send(t):
        for j in tile_owners(t):

            @pl.when(j != own)
            def _():
                remote(send_a.at[j], recv_a.at[own], sa.at[j], ra.at[own], member(j)).start()

    @pl.loop(0, 2)
    def _(n):
        tile_states(tile_at(TILES - 1 - n))

    pl.semaphore_wait(barrier, GROUP + DEPTH - 2)
    tile_send(tile_at(3))
    tile_send(tile_at(2))

    @pl.loop(2, TILES)
    def _(n):
        tile_states(tile_at(TILES - 1 - n))
        tile_send(tile_at(TILES - 1 - n))

    recv_a[own] = send_a[own]

    def near(t):
        near_part(t, rate, res, u_ref, g_ref, wtab, vtab, htab, near_c, near_g)

    @pl.loop(0, 2)
    def _(t):
        near(t)

    block = pl.ds(pl.multiple_of((me % RUN) * LANES, LANES), LANES)
    lam8 = rate[pl.ds(pl.multiple_of(seg * HALF, HALF), HALF), block] * (1.0 / SEQ)
    lam = jnp.concatenate([lam8, lam8], axis=0)
    dec = jnp.exp(-lam * float(ROWS))
    span = float(ROWS * RUN)
    dec_g = jnp.exp(-lam * span)
    ahead = jnp.exp(-lam8 * (span * z.astype(F32)))
    behind = jnp.exp(-lam8 * (span * (DEPTH - 1 - z).astype(F32)))
    decs = [jnp.ones((MODES, LANES), F32)]
    for w in range(1, RUN):
        decs.append(decs[-1] * dec)
    zero = jnp.zeros((MODES, LANES), F32)
    for j in others:
        remote(send_a.at[j], recv_a.at[j], sa.at[j], ra.at[j], member(j)).wait_recv()

    def combine(carry, part, decay, length):
        s, q, bn, tn, gr, gw, front, dist = carry
        s_j, m_j, b_j, t_j, gr_j, gw_j = part
        db = front * b_j
        return (
            decay * s + s_j,
            decay * (q + length * s) + m_j,
            bn + db,
            tn + front * t_j + dist * db,
            gr + gr_j + b_j * s,
            gw + gw_j + t_j * s + b_j * q,
            front * decay,
            dist + length,
        )

    ones = jnp.ones((MODES, LANES), F32)
    total = (zero, zero, zero, zero, zero, zero, ones, 0.0)
    nears = []
    for w in range(RUN):
        got = [recv_a[x * RUN + w].astype(F32) for x in range(SEGS)]
        part = [
            jnp.concatenate([rows[n * HALF : (n + 1) * HALF] for rows in got], axis=0) for n in range(6)
        ]
        pre_s[w] = total[0]
        nears.append(part[2])
        total = combine(total, part, dec, float(ROWS))
    s, q, bn, tn, gr, gw = total[:6]
    send_m[0:MODES, :] = s
    send_m[MODES : 2 * MODES, :] = bn
    send_x[...] = jnp.concatenate([q, tn, gr, gw], axis=0).astype(BF16)

    for p in layers:
        remote(send_m, recv_m.at[z], sm.at[p], rm.at[z], layer(p)).start()
    for p in layers:
        remote(send_x, recv_x.at[z], sx.at[p], rx.at[z], layer(p)).start()
    recv_m[z] = send_m[...]
    recv_x[z] = send_x[...]
    back = zero
    for w in reversed(range(RUN)):
        pre_b[w] = back
        back = dec * back + nears[w]

    @pl.loop(2, TILES)
    def _(t):
        near(t)

    for p in layers:
        remote(send_m, recv_m.at[p], sm.at[p], rm.at[p], layer(p)).wait_recv()
    state, whole = zero, zero
    for p in range(DEPTH):
        s_p = recv_m[p, 0:MODES, :]
        state = jnp.where(p < z, dec_g * state + s_p, state)
        whole = dec_g * whole + s_p
    state = jnp.concatenate([state[:HALF], state[HALF:] + ahead * whole[:HALF]], axis=0)
    back, whole = zero, zero
    for p in reversed(range(DEPTH)):
        b_p = recv_m[p, MODES : 2 * MODES, :]
        back = jnp.where(p > z, dec_g * back + b_p, back)
        whole = dec_g * whole + b_p
    back = jnp.concatenate([back[:HALF] + behind * whole[HALF:], back[HALF:]], axis=0)

    for w in range(RUN):
        st = pre_s[w] + decs[w] * state
        bk = pre_b[w] + decs[RUN - 1 - w] * back
        for x in range(SEGS):
            rows = slice(x * HALF, (x + 1) * HALF)
            send_c[x * RUN + w] = jnp.concatenate([st[rows], bk[rows]], axis=0)
    for j in others:
        remote(send_c.at[j], recv_c.at[own], sc.at[j], rc.at[own], member(j)).start()
    recv_c[own] = send_c[own]

    for p in layers:
        remote(send_x, recv_x.at[p], sx.at[p], rx.at[p], layer(p)).wait_recv()
    total = (zero, zero, zero, zero, zero, zero, ones, 0.0)
    for p in range(DEPTH):
        rest = recv_x[p].astype(F32)
        m_p, t_p, gr_p, gw_p = [rest[n * MODES : (n + 1) * MODES] for n in range(4)]
        part = (recv_m[p, 0:MODES, :], m_p, recv_m[p, MODES : 2 * MODES, :], t_p, gr_p, gw_p)
        total = combine(total, part, dec_g, span)
    s, q, bn, tn, gr, gw = total[:6]
    early, late = slice(0, HALF), slice(HALF, MODES)
    gr_all = gr[early] + gr[late] + bn[late] * s[early]
    gw_all = gw[early] + gw[late] + tn[late] * s[early] + bn[late] * q[early]
    send_e[...] = jnp.concatenate([gr_all, gw_all], axis=0).astype(BF16)
    for j in others:
        remote(send_e, recv_e.at[own], se.at[j], re.at[own], member(j)).start()
    recv_e[own] = send_e[...]

    results = ((gq, gq_hbm), (gk, gk_hbm), (gv, gv_hbm))

    def store(t, n):
        src, dst = results[n]
        return pltpu.make_async_copy(src.at[:, columns(t)], dst.at[:, columns(t)], out_sem.at[t, n])

    @pl.loop(0, TILES)
    def _(n):
        t = tile_at(n)
        for j in tile_owners(t):

            @pl.when(j != own)
            def _():
                remote(send_c.at[j], recv_c.at[j], sc.at[j], rc.at[j], member(j)).wait_recv()

        far_part(t, rate, res, k_in, v_in, go_in, wtab, vtab, sub_s, sub_b, near_c, near_g, recv_c, gq, gk, gv)
        for i in range(3):
            store(t, i).start()

    for j in others:
        remote(send_e, recv_e.at[j], se.at[j], re.at[j], member(j)).wait_recv()
    scale = SEQ ** -0.5
    for w in range(RUN):
        cols = slice(w * LANES, (w + 1) * LANES)
        got = [recv_e[x * RUN + w].astype(F32) for x in range(SEGS)]
        gr, gw = [
            jnp.concatenate([rows[n * HALF : (n + 1) * HALF] for rows in got], axis=0) for n in range(2)
        ]
        gres[:, cols] = scale * gr
        grate[:, cols] = (-scale / SEQ) * res[:, cols] * gw
    sums = (
        pltpu.make_async_copy(gres, gres_hbm, par_sem.at[0]),
        pltpu.make_async_copy(grate, grate_hbm, par_sem.at[1]),
    )
    for cp in sums:
        cp.start()
    for j in others:
        remote(send_a.at[j], recv_a.at[j], sa.at[j], ra.at[j], member(j)).wait_send()
        remote(send_c.at[j], recv_c.at[j], sc.at[j], rc.at[j], member(j)).wait_send()
        remote(send_e, recv_e.at[j], se.at[j], re.at[j], member(j)).wait_send()
    for p in layers:
        remote(send_m, recv_m.at[p], sm.at[p], rm.at[p], layer(p)).wait_send()
        remote(send_x, recv_x.at[p], sx.at[p], rx.at[p], layer(p)).wait_send()
    for t in range(TILES):
        for n in range(3):
            store(t, n).wait()
    for cp in sums:
        cp.wait()


def store_kernel(*refs):
    srcs, dsts, held, sem_in, sem_out = refs[:5], refs[5:10], refs[10:15], refs[15], refs[16]
    loads = [pltpu.make_async_copy(s, h, sem_in.at[n]) for n, (s, h) in enumerate(zip(srcs, held))]
    stores = [pltpu.make_async_copy(h, d, sem_out.at[n]) for n, (h, d) in enumerate(zip(held, dsts))]
    for cp in loads:
        cp.start()
    for load, store in zip(loads, stores):
        load.wait()
        store.start()
    for cp in stores:
        cp.wait()


def local(query, key_in, value, grad_out, residue, rate):
    hbm = pl.BlockSpec(memory_space=pltpu.HBM)
    big = jax.ShapeDtypeStruct((ROWS, CHANS), BF16)
    small = jax.ShapeDtypeStruct((MODES, CHANS), F32)
    dma = pltpu.SemaphoreType.DMA

    def buf(*shape, dtype=F32):
        return pltpu.VMEM(shape, dtype)

    results = pl.pallas_call(
        main_kernel,
        out_shape=(big, big, big, small, small),
        in_specs=[hbm] * 6,
        out_specs=[hbm] * 5,
        scratch_shapes=[
            *[buf(ROWS, CHANS, dtype=BF16)] * 3,
            *[buf(MODES, CHANS)] * 2,
            *[buf(ROWS, CHANS, dtype=BF16)] * 4,
            *[buf(MODES, CHANS)] * 2,
            *[buf(ROWS, CHANS, dtype=BF16)] * 2,
            *[buf(HALVES, ROWS, LANES)] * 2,
            *[buf(MODES, SUB, CHANS, dtype=BF16)] * 2,
            *[buf(SEGS, SUB // 2, 2 * HALF, CHANS, dtype=BF16)] * 2,
            buf(SUB, SUB, TILE, dtype=BF16),
            *[buf(NSUB, MODES, CHANS)] * 2,
            *[buf(ROWS, CHANS)] * 2,
            *[buf(GROUP, 6 * HALF, LANES, dtype=BF16)] * 2,
            *[buf(RUN, MODES, LANES)] * 2,
            buf(2 * MODES, LANES), buf(DEPTH, 2 * MODES, LANES),
            buf(4 * MODES, LANES, dtype=BF16), buf(DEPTH, 4 * MODES, LANES, dtype=BF16),
            *[buf(GROUP, 2 * HALF, LANES)] * 2,
            buf(2 * HALF, LANES, dtype=BF16), buf(GROUP, 2 * HALF, LANES, dtype=BF16),
            dma((TILES, 4)), dma((2,)), dma((TILES, 3)),
            dma((GROUP,)), dma((GROUP,)), dma((DEPTH,)), dma((DEPTH,)), dma((DEPTH,)), dma((DEPTH,)),
            dma((GROUP,)), dma((GROUP,)), dma((GROUP,)), dma((GROUP,)),
        ],
        compiler_params=pltpu.CompilerParams(collective_id=0, has_side_effects=True, vmem_limit_bytes=VMEM_LIMIT),
        name="hyena",
    )(query, key_in, value, grad_out, residue, rate)

    return pl.pallas_call(
        store_kernel,
        out_shape=(big, big, big, small, small),
        in_specs=[hbm] * 5,
        out_specs=[hbm] * 5,
        scratch_shapes=[
            *[buf(ROWS, CHANS, dtype=BF16)] * 3,
            *[buf(MODES, CHANS)] * 2,
            dma((5,)),
            dma((5,)),
        ],
        compiler_params=pltpu.CompilerParams(vmem_limit_bytes=VMEM_LIMIT),
        name="store",
    )(*results)


def solution(mesh):
    big, small = P("ctx", "tp"), P(None, "tp")
    return jax.shard_map(
        local, mesh=mesh, in_specs=(big, big, big, big, small, small),
        out_specs=(big, big, big, small, small), check_vma=False,
    )
```

time: 40 us -> 36.5 us (0.912)
  Pallas kernels: 39.3 us -> 35.7 us
    pallas_call x1, Pallas kernels: 37 us -> 33.4 us  [local(): pl.pallas_call(main_kernel, out_shape=(big, big, big, small, small), in_s...]
where the time goes in v4:
time: 36.5 us; the launch traced here: 36.4 us
  Pallas kernels  35.7 us (98%)
  between operations  0.64 us (2%)
    pallas_call x1, Pallas kernels, local(): pl.pallas_call(main_kernel, out_shape=(big, big, big, small, small), in_s...  33.4 us
    pallas_call x1, Pallas kernels, local(): pl.pallas_call(store_kernel, out_shape=(big, big, big, small, small), in_...  2.3 us

profile of v4, /device:TPU:1, one launch (start us, length us, event | category | flops | bytes accessed | tf_op | source)
XLA Modules:
  0.0 36.4 jit_solution(15065056500155129098)
XLA Ops:
  0.6 33.4 %hyena.1 = (bf16[256,1024]{1,0:T(8,128)(2,1)}, bf16[256,1024]{1,0:T(8,128)(2,1)}, bf16[256,1024]{1,0:T(8,128)(2,1)}, f32[16,1024]{1,0:T(8,128)}, f32[16,1024]{1,0:T(8,128)}) custom-call(bf16[256,1024]{1,0:T(8,128)(2,1)} %q_hbm.1, bf16[256,1024]{1,0:T(8,128)(2,1)} %k_hbm.1, bf16[256,1024]{1,0:T(8,128)(2,1)} %v_hbm.1, bf16[256,1024]{1,0:T(8,128)(2,1)} %go_hbm.1, ...), custom_call_target="tpu_custom_call" | custom-call | tf_op jit(solution)/shard_map/hyena/pallas_call | solution.py:469
  34.1 2.3 %store.1 = (bf16[256,1024]{1,0:T(8,128)(2,1)}, bf16[256,1024]{1,0:T(8,128)(2,1)}, bf16[256,1024]{1,0:T(8,128)(2,1)}, f32[16,1024]{1,0:T(8,128)}, f32[16,1024]{1,0:T(8,128)}) custom-call(bf16[256,1024]{1,0:T(8,128)(2,1)} %get-tuple-element.10.refs_0_, bf16[256,1024]{1,0:T(8,128)(2,1)} %get-tuple-element.11.refs_1_, ...), custom_call_target="tpu_custom_call" | custom-call | tf_op jit(solution)/shard_map/store/pallas_call | solution.py:500

commit v5 on v4

--- a/solution.py
+++ b/solution.py
@@ -21,7 +21,7 @@
 DEPTH = 8
 GROUP = SEGS * RUN
 HALF = MODES // SEGS
-VMEM_LIMIT = 63 * 2**20
+VMEM_LIMIT = 40 * 2**20
 F32 = jnp.float32
 BF16 = jnp.bfloat16
 MESH = pl.DeviceIdType.MESH
@@ -185,31 +185,33 @@
 
 def main_kernel(
     q_hbm, k_hbm, v_hbm, go_hbm, res_hbm, rate_hbm,
-    gq_hbm, gk_hbm, gv_hbm, gres_hbm, grate_hbm,
-    gq, gk, gv, gres, grate, q_in, k_in, v_in, go_in, res, rate, u_ref, g_ref, uf, gf, ptab, btab, wtab, vtab, htab,
+    gq, gk, gv, gres, grate,
+    q_in, k_in, v_in, go_in, res, rate, u_ref, g_ref, uf, gf, ptab, btab, wtab, vtab, htab,
     sub_s, sub_b, near_c, near_g,
     send_a, recv_a, pre_s, pre_b, send_m, recv_m, send_x, recv_x, send_c, recv_c, send_e, recv_e,
-    in_sem, par_sem, out_sem, sa, ra, sm, rm, sx, rx, sc, rc, se, re,
+    in_sem, par_sem, sa, ra, sm, rm, sx, rx, sc, rc, se, re,
 ):
     me = lax.axis_index("ctx")
-    seg = me // (DEPTH * RUN)
-    z = (me // RUN) % DEPTH
-    y = (me % RUN) // 2
-    own = seg * RUN + me % RUN
-    others = [(own + d) % GROUP for d in (12, 4, 11, 5, 13, 3, 10, 6, 14, 2, 9, 7, 8, 15, 1)]
-    layers = [(z + d) % DEPTH for d in (4, 5, 3, 6, 2, 7, 1)]
+    seg = lax.div(me, DEPTH * RUN)
+    z = lax.rem(lax.div(me, RUN), DEPTH)
+    run = lax.rem(me, RUN)
+    y = lax.div(run, 2)
+    own = seg * RUN + run
+    others = [lax.rem(own + d, GROUP) for d in (12, 4, 11, 5, 13, 3, 10, 6, 14, 2, 9, 7, 8, 15, 1)]
+    layers = [lax.rem(z + d, DEPTH) for d in (4, 5, 3, 6, 2, 7, 1)]
+    here, column = z * RUN, seg * (DEPTH * RUN) + run
 
     def member(j):
-        return {"ctx": (j // RUN) * (DEPTH * RUN) + z * RUN + j % RUN}
+        return {"ctx": lax.div(j, RUN) * ((DEPTH - 1) * RUN) + here + j}
 
     def layer(p):
-        return {"ctx": seg * (DEPTH * RUN) + p * RUN + me % RUN}
+        return {"ctx": column + p * RUN}
 
     def gray(n):
-        return n + n // 2 - 2 * (n // 3)
+        return n + lax.div(n, 2) - 2 * lax.div(n, 3)
 
     def tile_at(n):
-        return (y + gray(n)) % TILES
+        return lax.rem(y + gray(jnp.int32(n)), TILES)
 
     pairs = ((q_hbm, q_in), (k_hbm, k_in), (v_hbm, v_in), (go_hbm, go_in))
 
@@ -237,6 +239,14 @@
         return pltpu.make_async_remote_copy(
             src_ref=src, dst_ref=dst, send_sem=ssem, recv_sem=rsem, device_id=target, device_id_type=MESH
         )
+
+    def arrived(dst, count, rsem):
+        part = dst.at[pl.ds(0, count)]
+        remote(part, part, sa, rsem, member(others[0])).wait_recv()
+
+    def departed(like, count, ssem):
+        part = like.at[pl.ds(0, count)]
+        remote(part, part, ssem, ra, member(others[0])).wait_send()
 
     for cp in params:
         cp.wait()
@@ -267,7 +277,7 @@
 
             @pl.when(j != own)
             def _():
-                remote(send_a.at[j], recv_a.at[own], sa.at[j], ra.at[own], member(j)).start()
+                remote(send_a.at[j], recv_a.at[own], sa, ra, member(j)).start()
 
     @pl.loop(0, 2)
     def _(n):
@@ -291,7 +301,7 @@
     def _(t):
         near(t)
 
-    block = pl.ds(pl.multiple_of((me % RUN) * LANES, LANES), LANES)
+    block = pl.ds(pl.multiple_of(run * LANES, LANES), LANES)
     lam8 = rate[pl.ds(pl.multiple_of(seg * HALF, HALF), HALF), block] * (1.0 / SEQ)
     lam = jnp.concatenate([lam8, lam8], axis=0)
     dec = jnp.exp(-lam * float(ROWS))
@@ -303,8 +313,7 @@
     for w in range(1, RUN):
         decs.append(decs[-1] * dec)
     zero = jnp.zeros((MODES, LANES), F32)
-    for j in others:
-        remote(send_a.at[j], recv_a.at[j], sa.at[j], ra.at[j], member(j)).wait_recv()
+    arrived(recv_a, GROUP - 1, ra)
 
     def combine(carry, part, decay, length):
         s, q, bn, tn, gr, gw, front, dist = carry
@@ -333,14 +342,14 @@
         nears.append(part[2])
         total = combine(total, part, dec, float(ROWS))
     s, q, bn, tn, gr, gw = total[:6]
-    send_m[0:MODES, :] = s
-    send_m[MODES : 2 * MODES, :] = bn
-    send_x[...] = jnp.concatenate([q, tn, gr, gw], axis=0).astype(BF16)
+    send_m[...] = jnp.concatenate([s, bn], axis=0).astype(BF16)
+    early, late = slice(0, HALF), slice(HALF, MODES)
+    send_x[...] = jnp.concatenate([q, tn, gr[early] + gr[late], gw[early] + gw[late]], axis=0).astype(BF16)
 
     for p in layers:
-        remote(send_m, recv_m.at[z], sm.at[p], rm.at[z], layer(p)).start()
+        remote(send_m, recv_m.at[z], sm, rm, layer(p)).start()
     for p in layers:
-        remote(send_x, recv_x.at[z], sx.at[p], rx.at[z], layer(p)).start()
+        remote(send_x, recv_x.at[z], sx, rx, layer(p)).start()
     recv_m[z] = send_m[...]
     recv_x[z] = send_x[...]
     back = zero
@@ -352,17 +361,16 @@
     def _(t):
         near(t)
 
-    for p in layers:
-        remote(send_m, recv_m.at[p], sm.at[p], rm.at[p], layer(p)).wait_recv()
+    arrived(recv_m, DEPTH - 1, rm)
     state, whole = zero, zero
     for p in range(DEPTH):
-        s_p = recv_m[p, 0:MODES, :]
+        s_p = recv_m[p, 0:MODES, :].astype(F32)
         state = jnp.where(p < z, dec_g * state + s_p, state)
         whole = dec_g * whole + s_p
     state = jnp.concatenate([state[:HALF], state[HALF:] + ahead * whole[:HALF]], axis=0)
     back, whole = zero, zero
     for p in reversed(range(DEPTH)):
-        b_p = recv_m[p, MODES : 2 * MODES, :]
+        b_p = recv_m[p, MODES : 2 * MODES, :].astype(F32)
         back = jnp.where(p > z, dec_g * back + b_p, back)
         whole = dec_g * whole + b_p
     back = jnp.concatenate([back[:HALF] + behind * whole[HALF:], back[HALF:]], axis=0)
@@ -374,31 +382,25 @@
             rows = slice(x * HALF, (x + 1) * HALF)
             send_c[x * RUN + w] = jnp.concatenate([st[rows], bk[rows]], axis=0)
     for j in others:
-        remote(send_c.at[j], recv_c.at[own], sc.at[j], rc.at[own], member(j)).start()
+        remote(send_c.at[j], recv_c.at[own], sc, rc.at[own], member(j)).start()
     recv_c[own] = send_c[own]
 
-    for p in layers:
-        remote(send_x, recv_x.at[p], sx.at[p], rx.at[p], layer(p)).wait_recv()
+    arrived(recv_x, DEPTH - 1, rx)
     total = (zero, zero, zero, zero, zero, zero, ones, 0.0)
+    plain = jnp.zeros((MODES, LANES), F32)
     for p in range(DEPTH):
+        states_p = recv_m[p].astype(F32)
         rest = recv_x[p].astype(F32)
-        m_p, t_p, gr_p, gw_p = [rest[n * MODES : (n + 1) * MODES] for n in range(4)]
-        part = (recv_m[p, 0:MODES, :], m_p, recv_m[p, MODES : 2 * MODES, :], t_p, gr_p, gw_p)
+        plain = plain + rest[2 * MODES : 3 * MODES]
+        part = (states_p[:MODES], rest[:MODES], states_p[MODES:], rest[MODES : 2 * MODES], zero, zero)
         total = combine(total, part, dec_g, span)
     s, q, bn, tn, gr, gw = total[:6]
-    early, late = slice(0, HALF), slice(HALF, MODES)
-    gr_all = gr[early] + gr[late] + bn[late] * s[early]
-    gw_all = gw[early] + gw[late] + tn[late] * s[early] + bn[late] * q[early]
+    gr_all = plain[early] + gr[early] + gr[late] + bn[late] * s[early]
+    gw_all = plain[late] + gw[early] + gw[late] + tn[late] * s[early] + bn[late] * q[early]
     send_e[...] = jnp.concatenate([gr_all, gw_all], axis=0).astype(BF16)
     for j in others:
-        remote(send_e, recv_e.at[own], se.at[j], re.at[own], member(j)).start()
+        remote(send_e, recv_e.at[own], se, re, member(j)).start()
     recv_e[own] = send_e[...]
-
-    results = ((gq, gq_hbm), (gk, gk_hbm), (gv, gv_hbm))
-
-    def store(t, n):
-        src, dst = results[n]
-        return pltpu.make_async_copy(src.at[:, columns(t)], dst.at[:, columns(t)], out_sem.at[t, n])
 
     @pl.loop(0, TILES)
     def _(n):
@@ -407,14 +409,11 @@
 
             @pl.when(j != own)
             def _():
-                remote(send_c.at[j], recv_c.at[j], sc.at[j], rc.at[j], member(j)).wait_recv()
+                remote(send_c.at[j], recv_c.at[j], sc, rc.at[j], member(j)).wait_recv()
 
         far_part(t, rate, res, k_in, v_in, go_in, wtab, vtab, sub_s, sub_b, near_c, near_g, recv_c, gq, gk, gv)
-        for i in range(3):
-            store(t, i).start()
-
-    for j in others:
-        remote(send_e, recv_e.at[j], se.at[j], re.at[j], member(j)).wait_recv()
+
+    arrived(recv_e, GROUP - 1, re)
     scale = SEQ ** -0.5
     for w in range(RUN):
         cols = slice(w * LANES, (w + 1) * LANES)
@@ -424,41 +423,25 @@
         ]
         gres[:, cols] = scale * gr
         grate[:, cols] = (-scale / SEQ) * res[:, cols] * gw
-    sums = (
-        pltpu.make_async_copy(gres, gres_hbm, par_sem.at[0]),
-        pltpu.make_async_copy(grate, grate_hbm, par_sem.at[1]),
-    )
-    for cp in sums:
+    departed(recv_a, GROUP - 1, sa)
+    departed(recv_m, DEPTH - 1, sm)
+    departed(recv_x, DEPTH - 1, sx)
+    departed(recv_c, GROUP - 1, sc)
+    departed(recv_e, GROUP - 1, se)
+
+
+def store_kernel(*refs):
+    srcs, dsts, sem = refs[:5], refs[5:10], refs[10]
+    copies = [pltpu.make_async_copy(s, d, sem.at[n]) for n, (s, d) in enumerate(zip(srcs, dsts))]
+    for cp in copies:
         cp.start()
-    for j in others:
-        remote(send_a.at[j], recv_a.at[j], sa.at[j], ra.at[j], member(j)).wait_send()
-        remote(send_c.at[j], recv_c.at[j], sc.at[j], rc.at[j], member(j)).wait_send()
-        remote(send_e, recv_e.at[j], se.at[j], re.at[j], member(j)).wait_send()
-    for p in layers:
-        remote(send_m, recv_m.at[p], sm.at[p], rm.at[p], layer(p)).wait_send()
-        remote(send_x, recv_x.at[p], sx.at[p], rx.at[p], layer(p)).wait_send()
-    for t in range(TILES):
-        for n in range(3):
-            store(t, n).wait()
-    for cp in sums:
-        cp.wait()
-
-
-def store_kernel(*refs):
-    srcs, dsts, held, sem_in, sem_out = refs[:5], refs[5:10], refs[10:15], refs[15], refs[16]
-    loads = [pltpu.make_async_copy(s, h, sem_in.at[n]) for n, (s, h) in enumerate(zip(srcs, held))]
-    stores = [pltpu.make_async_copy(h, d, sem_out.at[n]) for n, (h, d) in enumerate(zip(held, dsts))]
-    for cp in loads:
-        cp.start()
-    for load, store in zip(loads, stores):
-        load.wait()
-        store.start()
-    for cp in stores:
+    for cp in copies:
         cp.wait()
 
 
 def local(query, key_in, value, grad_out, residue, rate):
     hbm = pl.BlockSpec(memory_space=pltpu.HBM)
+    vmem = pl.BlockSpec(memory_space=pltpu.VMEM)
     big = jax.ShapeDtypeStruct((ROWS, CHANS), BF16)
     small = jax.ShapeDtypeStruct((MODES, CHANS), F32)
     dma = pltpu.SemaphoreType.DMA
@@ -466,14 +449,14 @@
     def buf(*shape, dtype=F32):
         return pltpu.VMEM(shape, dtype)
 
+    held = [pltpu.VMEM((ROWS, CHANS), BF16)] * 3 + [pltpu.VMEM((MODES, CHANS), F32)] * 2
+    args = [pltpu.with_memory_space_constraint(x, pltpu.HBM) for x in (query, key_in, value, grad_out, residue, rate)]
     results = pl.pallas_call(
         main_kernel,
-        out_shape=(big, big, big, small, small),
+        out_shape=held,
         in_specs=[hbm] * 6,
-        out_specs=[hbm] * 5,
+        out_specs=[vmem] * 5,
         scratch_shapes=[
-            *[buf(ROWS, CHANS, dtype=BF16)] * 3,
-            *[buf(MODES, CHANS)] * 2,
             *[buf(ROWS, CHANS, dtype=BF16)] * 4,
             *[buf(MODES, CHANS)] * 2,
             *[buf(ROWS, CHANS, dtype=BF16)] * 2,
@@ -485,32 +468,26 @@
             *[buf(ROWS, CHANS)] * 2,
             *[buf(GROUP, 6 * HALF, LANES, dtype=BF16)] * 2,
             *[buf(RUN, MODES, LANES)] * 2,
-            buf(2 * MODES, LANES), buf(DEPTH, 2 * MODES, LANES),
-            buf(4 * MODES, LANES, dtype=BF16), buf(DEPTH, 4 * MODES, LANES, dtype=BF16),
+            buf(2 * MODES, LANES, dtype=BF16), buf(DEPTH, 2 * MODES, LANES, dtype=BF16),
+            buf(3 * MODES, LANES, dtype=BF16), buf(DEPTH, 3 * MODES, LANES, dtype=BF16),
             *[buf(GROUP, 2 * HALF, LANES)] * 2,
             buf(2 * HALF, LANES, dtype=BF16), buf(GROUP, 2 * HALF, LANES, dtype=BF16),
-            dma((TILES, 4)), dma((2,)), dma((TILES, 3)),
-            dma((GROUP,)), dma((GROUP,)), dma((DEPTH,)), dma((DEPTH,)), dma((DEPTH,)), dma((DEPTH,)),
-            dma((GROUP,)), dma((GROUP,)), dma((GROUP,)), dma((GROUP,)),
+            dma((TILES, 4)), dma((2,)),
+            dma, dma, dma, dma, dma, dma, dma, dma((GROUP,)), dma, dma,
         ],
         compiler_params=pltpu.CompilerParams(collective_id=0, has_side_effects=True, vmem_limit_bytes=VMEM_LIMIT),
         name="hyena",
-    )(query, key_in, value, grad_out, residue, rate)
+    )(*args)
 
     return pl.pallas_call(
         store_kernel,
         out_shape=(big, big, big, small, small),
-        in_specs=[hbm] * 5,
+        in_specs=[vmem] * 5,
         out_specs=[hbm] * 5,
-        scratch_shapes=[
-            *[buf(ROWS, CHANS, dtype=BF16)] * 3,
-            *[buf(MODES, CHANS)] * 2,
-            dma((5,)),
-            dma((5,)),
-        ],
-        compiler_params=pltpu.CompilerParams(vmem_limit_bytes=VMEM_LIMIT),
+        scratch_shapes=[dma((5,))],
+        compiler_params=pltpu.CompilerParams(vmem_limit_bytes=8 * 2**20),
         name="store",
-    )(*results)
+    )(*[pltpu.with_memory_space_constraint(x, pltpu.VMEM) for x in results])
 
 
 def solution(mesh):

time: 36.5 us -> 31.6 us (0.87)
  Pallas kernels: 35.7 us -> 30.9 us
    pallas_call x1, Pallas kernels: 33.4 us -> 29.7 us  [local(): pl.pallas_call(main_kernel, out_shape=held, in_specs=[hbm] * 6, out_specs...]
    pallas_call x1, Pallas kernels: 2.3 us -> 1.22 us  [local(): pl.pallas_call(store_kernel, out_shape=(big, big, big, small, small), in_...]
where the time goes in v5:
time: 31.6 us; the launch traced here: 31.5 us
  Pallas kernels  30.9 us (98%)
  between operations  0.64 us (2%)
    pallas_call x1, Pallas kernels, local(): pl.pallas_call(main_kernel, out_shape=held, in_specs=[hbm] * 6, out_specs...  29.7 us
    pallas_call x1, Pallas kernels, local(): pl.pallas_call(store_kernel, out_shape=(big, big, big, small, small), in_...  1.22 us

profile of v5, /device:TPU:1, one launch (start us, length us, event | category | flops | bytes accessed | tf_op | source)
XLA Modules:
  0.0 31.5 jit_solution(5690049580141855036)
XLA Ops:
  0.6 29.7 %hyena.1 = (bf16[256,1024]{1,0:T(8,128)(2,1)S(1)}, bf16[256,1024]{1,0:T(8,128)(2,1)S(1)}, bf16[256,1024]{1,0:T(8,128)(2,1)S(1)}, f32[16,1024]{1,0:T(8,128)S(1)}, f32[16,1024]{1,0:T(8,128)S(1)}) custom-call(bf16[256,1024]{1,0:T(8,128)(2,1)} %q_hbm.1, bf16[256,1024]{1,0:T(8,128)(2,1)} %k_hbm.1, bf16[256,1024]{1,0:T(8,128)(2,1)} %v_hbm.1, ...), custom_call_target="tpu_custom_call" | custom-call | tf_op jit(solution)/shard_map/hyena/pallas_call | solution.py:454
  30.3 1.2 %store.1 = (bf16[256,1024]{1,0:T(8,128)(2,1)}, bf16[256,1024]{1,0:T(8,128)(2,1)}, bf16[256,1024]{1,0:T(8,128)(2,1)}, f32[16,1024]{1,0:T(8,128)}, f32[16,1024]{1,0:T(8,128)}) custom-call(bf16[256,1024]{1,0:T(8,128)(2,1)S(1)} %get-tuple-element.10.refs_0_, bf16[256,1024]{1,0:T(8,128)(2,1)S(1)} %get-tuple-element.11.refs_1_, ...), custom_call_target="tpu_custom_call" | custom-call | tf_op jit(solution)/shard_map/store/pallas_call | solution.py:482

commit v6 on v5

--- a/solution.py
+++ b/solution.py
@@ -147,7 +147,7 @@
     def incoming(n):
         rows = slice(n * HALF, (n + 1) * HALF)
         parts = [
-            jnp.concatenate([recv_c[x * RUN + t * HALVES + h, rows, :] for x in range(SEGS)], axis=0)
+            jnp.concatenate([recv_c[x * RUN + t * HALVES + h].astype(F32)[rows] for x in range(SEGS)], axis=0)
             for h in range(HALVES)
         ]
         return jnp.concatenate(parts, axis=1)
@@ -270,7 +270,7 @@
         states(t, rate, u_ref, g_ref, ptab, btab, uf, gf, sub_s, sub_b, send_a)
 
     def tile_owners(t):
-        return [x * RUN + t * HALVES + half for x in range(SEGS) for half in range(HALVES)]
+        return [x * RUN + t * HALVES + half for x in (1 - seg, seg) for half in range(HALVES)]
 
     def tile_send(t):
         for j in tile_owners(t):
@@ -331,31 +331,32 @@
         )
 
     ones = jnp.ones((MODES, LANES), F32)
+    s, bn = zero, zero
+    for w in range(RUN):
+        pre_s[w] = s
+        last = RUN - 1 - w
+        pre_b[last] = bn
+        s = dec * s + jnp.concatenate([recv_a[x * RUN + w].astype(F32)[0:HALF] for x in range(SEGS)], axis=0)
+        near_b = [recv_a[x * RUN + last].astype(F32)[2 * HALF : 3 * HALF] for x in range(SEGS)]
+        bn = dec * bn + jnp.concatenate(near_b, axis=0)
+    send_m[...] = jnp.concatenate([s, bn], axis=0).astype(BF16)
+    for p in layers:
+        remote(send_m, recv_m.at[z], sm, rm, layer(p)).start()
     total = (zero, zero, zero, zero, zero, zero, ones, 0.0)
-    nears = []
     for w in range(RUN):
         got = [recv_a[x * RUN + w].astype(F32) for x in range(SEGS)]
         part = [
             jnp.concatenate([rows[n * HALF : (n + 1) * HALF] for rows in got], axis=0) for n in range(6)
         ]
-        pre_s[w] = total[0]
-        nears.append(part[2])
         total = combine(total, part, dec, float(ROWS))
     s, q, bn, tn, gr, gw = total[:6]
-    send_m[...] = jnp.concatenate([s, bn], axis=0).astype(BF16)
     early, late = slice(0, HALF), slice(HALF, MODES)
     send_x[...] = jnp.concatenate([q, tn, gr[early] + gr[late], gw[early] + gw[late]], axis=0).astype(BF16)
 
-    for p in layers:
-        remote(send_m, recv_m.at[z], sm, rm, layer(p)).start()
     for p in layers:
         remote(send_x, recv_x.at[z], sx, rx, layer(p)).start()
     recv_m[z] = send_m[...]
     recv_x[z] = send_x[...]
-    back = zero
-    for w in reversed(range(RUN)):
-        pre_b[w] = back
-        back = dec * back + nears[w]
 
     @pl.loop(2, TILES)
     def _(t):
@@ -380,7 +381,7 @@
         bk = pre_b[w] + decs[RUN - 1 - w] * back
         for x in range(SEGS):
             rows = slice(x * HALF, (x + 1) * HALF)
-            send_c[x * RUN + w] = jnp.concatenate([st[rows], bk[rows]], axis=0)
+            send_c[x * RUN + w] = jnp.concatenate([st[rows], bk[rows]], axis=0).astype(BF16)
     for j in others:
         remote(send_c.at[j], recv_c.at[own], sc, rc.at[own], member(j)).start()
     recv_c[own] = send_c[own]
@@ -470,7 +471,7 @@
             *[buf(RUN, MODES, LANES)] * 2,
             buf(2 * MODES, LANES, dtype=BF16), buf(DEPTH, 2 * MODES, LANES, dtype=BF16),
             buf(3 * MODES, LANES, dtype=BF16), buf(DEPTH, 3 * MODES, LANES, dtype=BF16),
-            *[buf(GROUP, 2 * HALF, LANES)] * 2,
+            *[buf(GROUP, 2 * HALF, LANES, dtype=BF16)] * 2,
             buf(2 * HALF, LANES, dtype=BF16), buf(GROUP, 2 * HALF, LANES, dtype=BF16),
             dma((TILES, 4)), dma((2,)),
             dma, dma, dma, dma, dma, dma, dma, dma((GROUP,)), dma, dma,

time: 31.6 us -> 31.1 us (0.984)
  Pallas kernels: 30.9 us -> 30.3 us
    pallas_call x1, Pallas kernels: 29.7 us -> 29.1 us  [local(): pl.pallas_call(main_kernel, out_shape=held, in_specs=[hbm] * 6, out_specs...]
where the time goes in v6:
time: 31.1 us; the launch traced here: 31 us
  Pallas kernels  30.3 us (97%)
  between operations  0.64 us (2%)
    pallas_call x1, Pallas kernels, local(): pl.pallas_call(main_kernel, out_shape=held, in_specs=[hbm] * 6, out_specs...  29.1 us
    pallas_call x1, Pallas kernels, local(): pl.pallas_call(store_kernel, out_shape=(big, big, big, small, small), in_...  1.22 us

profile of v6, /device:TPU:1, one launch (start us, length us, event | category | flops | bytes accessed | tf_op | source)
XLA Modules:
  0.0 31.0 jit_solution(8972467792472346173)
XLA Ops:
  0.6 29.1 %hyena.1 = (bf16[256,1024]{1,0:T(8,128)(2,1)S(1)}, bf16[256,1024]{1,0:T(8,128)(2,1)S(1)}, bf16[256,1024]{1,0:T(8,128)(2,1)S(1)}, f32[16,1024]{1,0:T(8,128)S(1)}, f32[16,1024]{1,0:T(8,128)S(1)}) custom-call(bf16[256,1024]{1,0:T(8,128)(2,1)} %q_hbm.1, bf16[256,1024]{1,0:T(8,128)(2,1)} %k_hbm.1, bf16[256,1024]{1,0:T(8,128)(2,1)} %v_hbm.1, ...), custom_call_target="tpu_custom_call" | custom-call | tf_op jit(solution)/shard_map/hyena/pallas_call | solution.py:455
  29.8 1.2 %store.1 = (bf16[256,1024]{1,0:T(8,128)(2,1)}, bf16[256,1024]{1,0:T(8,128)(2,1)}, bf16[256,1024]{1,0:T(8,128)(2,1)}, f32[16,1024]{1,0:T(8,128)}, f32[16,1024]{1,0:T(8,128)}) custom-call(bf16[256,1024]{1,0:T(8,128)(2,1)S(1)} %get-tuple-element.10.refs_0_, bf16[256,1024]{1,0:T(8,128)(2,1)S(1)} %get-tuple-element.11.refs_1_, ...), custom_call_target="tpu_custom_call" | custom-call | tf_op jit(solution)/shard_map/store/pallas_call | solution.py:483

commit v7 on v6

--- a/solution.py
+++ b/solution.py
@@ -225,15 +225,15 @@
     )
     for cp in params:
         cp.start()
+    barrier = pltpu.get_barrier_semaphore()
+    for p in layers:
+        pl.semaphore_signal(barrier, inc=1, device_id=layer(p), device_id_type=MESH)
+    for j in others:
+        pl.semaphore_signal(barrier, inc=1, device_id=member(j), device_id_type=MESH)
+
     for n in reversed(range(TILES)):
         for i in range(4):
             load(tile_at(n), i).start()
-
-    barrier = pltpu.get_barrier_semaphore()
-    for j in others:
-        pl.semaphore_signal(barrier, inc=1, device_id=member(j), device_id_type=MESH)
-    for p in layers:
-        pl.semaphore_signal(barrier, inc=1, device_id=layer(p), device_id_type=MESH)
 
     def remote(src, dst, ssem, rsem, target):
         return pltpu.make_async_remote_copy(

time: 31.1 us -> 30.8 us (level)
    pallas_call x1, Pallas kernels: 29.1 us -> 28.8 us  [local(): pl.pallas_call(main_kernel, out_shape=held, in_specs=[hbm] * 6, out_specs...]
where the time goes in v7:
time: 30.8 us; the launch traced here: 30.7 us
  Pallas kernels  30 us (97%)
  between operations  0.64 us (2%)
    pallas_call x1, Pallas kernels, local(): pl.pallas_call(main_kernel, out_shape=held, in_specs=[hbm] * 6, out_specs...  28.8 us
    pallas_call x1, Pallas kernels, local(): pl.pallas_call(store_kernel, out_shape=(big, big, big, small, small), in_...  1.22 us

profile of v7, /device:TPU:1, one launch (start us, length us, event | category | flops | bytes accessed | tf_op | source)
XLA Modules:
  0.0 30.7 jit_solution(11572760481504382541)
XLA Ops:
  0.6 28.8 %hyena.1 = (bf16[256,1024]{1,0:T(8,128)(2,1)S(1)}, bf16[256,1024]{1,0:T(8,128)(2,1)S(1)}, bf16[256,1024]{1,0:T(8,128)(2,1)S(1)}, f32[16,1024]{1,0:T(8,128)S(1)}, f32[16,1024]{1,0:T(8,128)S(1)}) custom-call(bf16[256,1024]{1,0:T(8,128)(2,1)} %q_hbm.1, bf16[256,1024]{1,0:T(8,128)(2,1)} %k_hbm.1, bf16[256,1024]{1,0:T(8,128)(2,1)} %v_hbm.1, ...), custom_call_target="tpu_custom_call" | custom-call | tf_op jit(solution)/shard_map/hyena/pallas_call | solution.py:455
  29.4 1.2 %store.1 = (bf16[256,1024]{1,0:T(8,128)(2,1)}, bf16[256,1024]{1,0:T(8,128)(2,1)}, bf16[256,1024]{1,0:T(8,128)(2,1)}, f32[16,1024]{1,0:T(8,128)}, f32[16,1024]{1,0:T(8,128)}) custom-call(bf16[256,1024]{1,0:T(8,128)(2,1)S(1)} %get-tuple-element.10.refs_0_, bf16[256,1024]{1,0:T(8,128)(2,1)S(1)} %get-tuple-element.11.refs_1_, ...), custom_call_target="tpu_custom_call" | custom-call | tf_op jit(solution)/shard_map/store/pallas_call | solution.py:483

commit v8 on v7

--- a/solution.py
+++ b/solution.py
@@ -53,24 +53,30 @@
         btab[m, :, cols] = jnp.exp(-row * (pos + 1.0)).astype(BF16)
 
 
-def states(t, rate, u_ref, g_ref, ptab, btab, uf, gf, sub_s, sub_b, send_a):
-    cols = columns(t)
-    lam = rate[:, cols] * (1.0 / SEQ)
+def selectors(sel_s, sel_b, pick):
     out_row = iota((2 * MODES, MODES * SUB), 0)
     in_row = iota((2 * MODES, MODES * SUB), 1)
     hit = (in_row // SUB) == (out_row % MODES)
     off = (in_row % SUB).astype(F32)
     first = out_row < MODES
-    sel_s = jnp.where(hit, jnp.where(first, 1.0, SUB - 1.0 - off), 0.0).astype(BF16)
-    sel_b = jnp.where(hit, jnp.where(first, 1.0, off + 1.0), 0.0).astype(BF16)
+    sel_s[...] = jnp.where(hit, jnp.where(first, 1.0, SUB - 1.0 - off), 0.0).astype(BF16)
+    sel_b[...] = jnp.where(hit, jnp.where(first, 1.0, off + 1.0), 0.0).astype(BF16)
+    out_row = iota((2 * SUB, SUB * MODES), 0)
+    in_row = iota((2 * SUB, SUB * MODES), 1)
+    pick[...] = jnp.where(in_row // HALF == out_row, 1.0, 0.0).astype(BF16)
+
+
+def states(t, rate, u_ref, g_ref, ptab, btab, sel_s, sel_b, uf, gf, sub_s, sub_b, send_a):
+    cols = columns(t)
+    lam = rate[:, cols] * (1.0 / SEQ)
     step = jnp.exp(-lam * SUB)
     zero = jnp.zeros((MODES, TILE), F32)
     s, q, bn, tn, gr, gw = zero, zero, zero, zero, zero, zero
     decay = jnp.ones((MODES, TILE), F32)
     for k in range(NSUB):
         rows = slice(k * SUB, (k + 1) * SUB)
-        su = dot(sel_s, spread(ptab[:, :, cols], u_ref[rows, cols]))
-        sg = dot(sel_b, spread(btab[:, :, cols], g_ref[rows, cols]))
+        su = dot(sel_s[...], spread(ptab[:, :, cols], u_ref[rows, cols]))
+        sg = dot(sel_b[...], spread(btab[:, :, cols], g_ref[rows, cols]))
         s_k, m_k = su[:MODES], su[MODES:]
         b_k, t_k = sg[:MODES], sg[MODES:]
         sub_s[k, :, cols] = s_k
@@ -138,7 +144,7 @@
         near_g[rows, cols] = dot(up, spread(htab[...], g_ref[rows, cols]))
 
 
-def far_part(t, rate, res, k_in, v_in, go_in, wtab, vtab, sub_s, sub_b, near_c, near_g, recv_c, gq, gk, gv):
+def far_part(t, rate, res, pick, k_in, v_in, go_in, wtab, vtab, sub_s, sub_b, near_c, near_g, recv_c, gq, gk, gv):
     cols = columns(t)
     lam = rate[:, cols] * (1.0 / SEQ)
     step = jnp.exp(-lam * SUB)
@@ -151,10 +157,6 @@
             for h in range(HALVES)
         ]
         return jnp.concatenate(parts, axis=1)
-
-    out_row = iota((2 * SUB, SUB * MODES), 0)
-    in_row = iota((2 * SUB, SUB * MODES), 1)
-    pick = jnp.where(in_row // HALF == out_row, 1.0, 0.0).astype(BF16)
 
     def reach(tab, xs):
         sums = []
@@ -164,7 +166,7 @@
             low = jnp.concatenate([x[:HALF], x[:HALF]], axis=0).astype(BF16)
             high = jnp.concatenate([x[HALF:], x[HALF:]], axis=0).astype(BF16)
             sums.append((tab[0, :, :, cols] * low[None] + tab[1, :, :, cols] * high[None]).reshape(SUB * HALF, TILE))
-        return dot(pick, jnp.concatenate(sums, axis=0)) + jnp.concatenate(bases, axis=0)
+        return dot(pick[...], jnp.concatenate(sums, axis=0)) + jnp.concatenate(bases, axis=0)
 
     x = incoming(0)
     for k in range(0, NSUB, 2):
@@ -186,7 +188,7 @@
 def main_kernel(
     q_hbm, k_hbm, v_hbm, go_hbm, res_hbm, rate_hbm,
     gq, gk, gv, gres, grate,
-    q_in, k_in, v_in, go_in, res, rate, u_ref, g_ref, uf, gf, ptab, btab, wtab, vtab, htab,
+    q_in, k_in, v_in, go_in, res, rate, u_ref, g_ref, uf, gf, ptab, btab, wtab, vtab, htab, sel_s, sel_b, pick,
     sub_s, sub_b, near_c, near_g,
     send_a, recv_a, pre_s, pre_b, send_m, recv_m, send_x, recv_x, send_c, recv_c, send_e, recv_e,
     in_sem, par_sem, sa, ra, sm, rm, sx, rx, sc, rc, se, re,
@@ -248,6 +250,7 @@
         part = like.at[pl.ds(0, count)]
         remote(part, part, ssem, ra, member(others[0])).wait_send()
 
+    selectors(sel_s, sel_b, pick)
     for cp in params:
         cp.wait()
 
@@ -267,7 +270,7 @@
             part = slice(half * LANES, (half + 1) * LANES)
             uf[half] = u[:, part].astype(F32)
             gf[half] = g[:, part].astype(F32)
-        states(t, rate, u_ref, g_ref, ptab, btab, uf, gf, sub_s, sub_b, send_a)
+        states(t, rate, u_ref, g_ref, ptab, btab, sel_s, sel_b, uf, gf, sub_s, sub_b, send_a)
 
     def tile_owners(t):
         return [x * RUN + t * HALVES + half for x in (1 - seg, seg) for half in range(HALVES)]
@@ -382,7 +385,7 @@
         for x in range(SEGS):
             rows = slice(x * HALF, (x + 1) * HALF)
             send_c[x * RUN + w] = jnp.concatenate([st[rows], bk[rows]], axis=0).astype(BF16)
-    for j in others:
+    for j in reversed(others):
         remote(send_c.at[j], recv_c.at[own], sc, rc.at[own], member(j)).start()
     recv_c[own] = send_c[own]
 
@@ -412,7 +415,7 @@
             def _():
                 remote(send_c.at[j], recv_c.at[j], sc, rc.at[j], member(j)).wait_recv()
 
-        far_part(t, rate, res, k_in, v_in, go_in, wtab, vtab, sub_s, sub_b, near_c, near_g, recv_c, gq, gk, gv)
+        far_part(t, rate, res, pick, k_in, v_in, go_in, wtab, vtab, sub_s, sub_b, near_c, near_g, recv_c, gq, gk, gv)
 
     arrived(recv_e, GROUP - 1, re)
     scale = SEQ ** -0.5
@@ -465,6 +468,7 @@
             *[buf(MODES, SUB, CHANS, dtype=BF16)] * 2,
             *[buf(SEGS, SUB // 2, 2 * HALF, CHANS, dtype=BF16)] * 2,
             buf(SUB, SUB, TILE, dtype=BF16),
+            *[buf(2 * MODES, MODES * SUB, dtype=BF16)] * 3,
             *[buf(NSUB, MODES, CHANS)] * 2,
             *[buf(ROWS, CHANS)] * 2,
             *[buf(GROUP, 6 * HALF, LANES, dtype=BF16)] * 2,

time: 30.8 us -> 30.6 us (level)
  no operation moved by 1% of the time
where the time goes in v8:
time: 30.6 us; the launch traced here: 30.5 us
  Pallas kernels  29.9 us (98%)
  between operations  0.64 us (2%)
    pallas_call x1, Pallas kernels, local(): pl.pallas_call(main_kernel, out_shape=held, in_specs=[hbm] * 6, out_specs...  28.6 us
    pallas_call x1, Pallas kernels, local(): pl.pallas_call(store_kernel, out_shape=(big, big, big, small, small), in_...  1.22 us

profile of v8, /device:TPU:1, one launch (start us, length us, event | category | flops | bytes accessed | tf_op | source)
XLA Modules:
  0.0 30.5 jit_solution(6821278732901225530)
XLA Ops:
  0.6 28.6 %hyena.1 = (bf16[256,1024]{1,0:T(8,128)(2,1)S(1)}, bf16[256,1024]{1,0:T(8,128)(2,1)S(1)}, bf16[256,1024]{1,0:T(8,128)(2,1)S(1)}, f32[16,1024]{1,0:T(8,128)S(1)}, f32[16,1024]{1,0:T(8,128)S(1)}) custom-call(bf16[256,1024]{1,0:T(8,128)(2,1)} %q_hbm.1, bf16[256,1024]{1,0:T(8,128)(2,1)} %k_hbm.1, bf16[256,1024]{1,0:T(8,128)(2,1)} %v_hbm.1, ...), custom_call_target="tpu_custom_call" | custom-call | tf_op jit(solution)/shard_map/hyena/pallas_call | solution.py:458
  29.3 1.2 %store.1 = (bf16[256,1024]{1,0:T(8,128)(2,1)}, bf16[256,1024]{1,0:T(8,128)(2,1)}, bf16[256,1024]{1,0:T(8,128)(2,1)}, f32[16,1024]{1,0:T(8,128)}, f32[16,1024]{1,0:T(8,128)}) custom-call(bf16[256,1024]{1,0:T(8,128)(2,1)S(1)} %get-tuple-element.10.refs_0_, bf16[256,1024]{1,0:T(8,128)(2,1)S(1)} %get-tuple-element.11.refs_1_, ...), custom_call_target="tpu_custom_call" | custom-call | tf_op jit(solution)/shard_map/store/pallas_call | solution.py:487

commit v9 on v8

--- a/solution.py
+++ b/solution.py
@@ -385,7 +385,7 @@
         for x in range(SEGS):
             rows = slice(x * HALF, (x + 1) * HALF)
             send_c[x * RUN + w] = jnp.concatenate([st[rows], bk[rows]], axis=0).astype(BF16)
-    for j in reversed(others):
+    for j in others:
         remote(send_c.at[j], recv_c.at[own], sc, rc.at[own], member(j)).start()
     recv_c[own] = send_c[own]
 

time: 30.6 us -> 30.7 us (level)
  no operation moved by 1% of the time
where the time goes in v9:
time: 30.7 us; the launch traced here: 30.6 us
  Pallas kernels  30 us (98%)
  between operations  0.64 us (2%)
    pallas_call x1, Pallas kernels, local(): pl.pallas_call(main_kernel, out_shape=held, in_specs=[hbm] * 6, out_specs...  28.8 us
    pallas_call x1, Pallas kernels, local(): pl.pallas_call(store_kernel, out_shape=(big, big, big, small, small), in_...  1.22 us

profile of v9, /device:TPU:1, one launch (start us, length us, event | category | flops | bytes accessed | tf_op | source)
XLA Modules:
  0.0 30.6 jit_solution(11502210481536234306)
XLA Ops:
  0.6 28.8 %hyena.1 = (bf16[256,1024]{1,0:T(8,128)(2,1)S(1)}, bf16[256,1024]{1,0:T(8,128)(2,1)S(1)}, bf16[256,1024]{1,0:T(8,128)(2,1)S(1)}, f32[16,1024]{1,0:T(8,128)S(1)}, f32[16,1024]{1,0:T(8,128)S(1)}) custom-call(bf16[256,1024]{1,0:T(8,128)(2,1)} %q_hbm.1, bf16[256,1024]{1,0:T(8,128)(2,1)} %k_hbm.1, bf16[256,1024]{1,0:T(8,128)(2,1)} %v_hbm.1, ...), custom_call_target="tpu_custom_call" | custom-call | tf_op jit(solution)/shard_map/hyena/pallas_call | solution.py:458
  29.4 1.2 %store.1 = (bf16[256,1024]{1,0:T(8,128)(2,1)}, bf16[256,1024]{1,0:T(8,128)(2,1)}, bf16[256,1024]{1,0:T(8,128)(2,1)}, f32[16,1024]{1,0:T(8,128)}, f32[16,1024]{1,0:T(8,128)}) custom-call(bf16[256,1024]{1,0:T(8,128)(2,1)S(1)} %get-tuple-element.10.refs_0_, bf16[256,1024]{1,0:T(8,128)(2,1)S(1)} %get-tuple-element.11.refs_1_, ...), custom_call_target="tpu_custom_call" | custom-call | tf_op jit(solution)/shard_map/store/pallas_call | solution.py:487
